TPU v7x, 256 devices: a whole 4x4x8 slice. The times are simulated.
256 devices in a mesh: dp: 2 (over x_lo), ctx: 32 (over z, y), head: 4 (over x_hi, core).
Axes of the slice: x: 4 (x_hi: 2, x_lo: 2; x = x_hi * 2 + x_lo), y: 4, z: 8, core: 2. Of those that a mesh axis runs over, the one named last changes fastest.
Arguments:
- queries: bfloat16 [16384, 4096], P(('dp', 'ctx'), 'head'), parts along dimension 0, may hold values from -100 to 100
- keys: bfloat16 [16384, 1024], P(('dp', 'ctx'), 'head'), parts along dimension 0, may hold values from -13 to 13
- values: bfloat16 [16384, 1024], P(('dp', 'ctx'), 'head'), parts along dimension 0, may hold values from -6 to 6
- latents: bfloat16 [512, 4096], P(None, 'head'), may hold values from -400 to 400
- norm_gain: float32 [4096], P('head'), may hold values from 0.1 to 1.9
- block_doc: int32 [128], P('dp'), parts along dimension 0, may hold values from 0 to 15, as said below
- block_source: int32 [128], P('dp'), parts along dimension 0, may hold values from 0 to 63, as said below
Outputs:
- attended: bfloat16 [16384, 4096], P(('dp', 'ctx'), 'head'), parts along dimension 0
- embeddings: float32 [32, 4096], P('dp', 'head'), parts along dimension 0
There are 2 independent parts, one for each index of `dp`. A program takes and returns all parts, laid end to end along the dimension named above; an argument that names none is the same for every part. Nothing has to cross between parts.
Inputs may be any that keep to these rules, and one draw needn't show every extreme that they name: `block_doc`: documents are whole runs of blocks in increasing id order; every document has one or more blocks and one has exactly 40. block_source is a permutation of the 64 blocks.
All inputs are finite; a program needn't handle non-finite values.
Results may differ from a plain program's by a relative error of at most 0.011.
Values may be sent and summed in bfloat16 or wider, within the bound.
A program may use at most 128 MiB of HBM per device.

v0:
```python
import math

import jax
import jax.numpy as jnp
from jax import lax
from jax.sharding import PartitionSpec as P

HEADS = 32
HEAD_DIM = 128
POOL_HEADS = 8
BLOCK = 128


def shards(queries, keys, values, latents, norm_gain, block_doc, block_source):
    tok_dev = queries.shape[0]
    columns = queries.shape[1]
    kv_dev = keys.shape[1] // HEAD_DIM
    group_size = columns // HEAD_DIM // kv_dev
    shard_at = lax.axis_index("ctx")
    n_docs = block_doc.shape[0] // 4
    blocks_dev = tok_dev // BLOCK
    score_scale = HEAD_DIM ** (-0.5)
    offsets = jnp.arange(BLOCK, dtype=jnp.int32)
    token_doc = jnp.repeat(block_doc, BLOCK)
    sources = lax.dynamic_slice_in_dim(block_source, shard_at * blocks_dev, blocks_dev)
    moved_doc = jnp.repeat(jnp.take(block_doc, sources), BLOCK)
    source_rows = (sources[:, None] * BLOCK + offsets[None, :]).reshape(-1)
    piece = lax.all_gather(queries, "ctx", axis=0, tiled=True)
    piece_rows = piece.shape[0]
    inside = (source_rows >= 0) & (source_rows < piece_rows)
    taken = jnp.take(piece, jnp.clip(source_rows, 0, piece_rows - 1), axis=0)
    moved_queries = jnp.where(inside[:, None], taken, jnp.zeros_like(queries))
    rows_here = moved_queries.shape[0]
    query_heads = moved_queries.reshape(rows_here, kv_dev, group_size, HEAD_DIM)
    initial = (
        jnp.full((rows_here, kv_dev, group_size), -1e30, jnp.float32),
        jnp.zeros((rows_here, kv_dev, group_size), jnp.float32),
        jnp.zeros((rows_here, kv_dev, group_size, HEAD_DIM), jnp.float32),
    )

    def add_tile(carried, key_piece, value_piece, key_doc):
        same_doc = moved_doc[:, None] == key_doc[None, :]
        key_heads = key_piece.reshape(-1, kv_dev, HEAD_DIM)
        value_heads = value_piece.reshape(-1, kv_dev, HEAD_DIM)
        running_max, running_sum, weighted = carried
        scores = (
            jnp.einsum("nkgd,mkd->nkgm", query_heads, key_heads, preferred_element_type=jnp.float32)
            * score_scale
        )
        visible = same_doc[:, None, None, :]
        scores = jnp.where(visible, scores, -1e30)
        new_max = jnp.maximum(running_max, jnp.max(scores, axis=-1))
        weights = jnp.where(visible, jnp.exp(scores - new_max[..., None]), 0.0)
        rescale = jnp.exp(running_max - new_max)
        running_sum = running_sum * rescale + jnp.sum(weights, axis=-1)
        weighted = weighted * rescale[..., None] + jnp.einsum(
            "nkgm,mkd->nkgd",
            weights.astype(jnp.bfloat16),
            value_heads,
            preferred_element_type=jnp.float32,
        )
        return (new_max, running_sum, weighted)

    key_piece = lax.all_gather(keys, "ctx", axis=0, tiled=True)
    value_piece = lax.all_gather(values, "ctx", axis=0, tiled=True)
    piece_rows = key_piece.shape[0]
    tile_rows = math.gcd(piece_rows, 512)
    tile_count = piece_rows // tile_rows
    key_doc = token_doc

    def scan_step(state, pieces):
        return (add_tile(state, pieces[0], pieces[1], pieces[2]), None)

    result, _ = lax.scan(
        scan_step,
        initial,
        (
            key_piece.reshape(tile_count, tile_rows, -1),
            value_piece.reshape(tile_count, tile_rows, -1),
            key_doc.reshape(tile_count, tile_rows),
        ),
    )
    running_max, running_sum, weighted = result
    attended = (weighted / running_sum[..., None]).reshape(rows_here, columns).astype(jnp.bfloat16)
    as_float = attended.astype(jnp.float32)
    squares = jnp.sum(as_float * as_float, axis=-1)
    channel_total = lax.psum(squares, "head")
    normed = (
        as_float * lax.rsqrt(channel_total / (HEADS * HEAD_DIM) + 1e-05)[:, None] * norm_gain
    ).astype(jnp.bfloat16)
    pool_dev = POOL_HEADS // lax.axis_size("head")
    pool_width = columns // pool_dev
    pooled_parts = []
    for pool_head in range(pool_dev):
        normed_head = normed[:, pool_head * pool_width : (pool_head + 1) * pool_width]
        latent_head = latents[:, pool_head * pool_width : (pool_head + 1) * pool_width]
        scores = lax.dot_general(
            normed_head, latent_head, (((1,), (1,)), ((), ())), preferred_element_type=jnp.float32
        ) * pool_width ** (-0.5)
        peak = jnp.max(scores, axis=-1, keepdims=True)
        weights = jnp.exp(scores - peak)
        weights = weights / jnp.sum(weights, axis=-1, keepdims=True)
        pooled_parts.append(
            jnp.dot(weights.astype(jnp.bfloat16), latent_head, preferred_element_type=jnp.float32)
        )
    pooled = jnp.concatenate(pooled_parts, axis=1)
    one_hot = (moved_doc[:, None] == jnp.arange(n_docs, dtype=jnp.int32)[None, :]).astype(
        jnp.float32
    )
    local_sums = lax.dot_general(
        one_hot,
        pooled,
        (((0,), (0,)), ((), ())),
        precision=lax.Precision.HIGHEST,
        preferred_element_type=jnp.float32,
    )
    doc_sums = lax.psum(local_sums.astype(jnp.bfloat16), "ctx").astype(jnp.float32)
    doc_squares = jnp.sum(doc_sums * doc_sums, axis=-1)
    doc_total = lax.psum(doc_squares, "head")
    embedded = doc_sums * lax.rsqrt(doc_total / (HEADS * HEAD_DIM) + 1e-05)[:, None]
    return (attended, embedded)


def solution(mesh):
    in_specs = (
        P(("dp", "ctx"), "head"),
        P(("dp", "ctx"), "head"),
        P(("dp", "ctx"), "head"),
        P(None, "head"),
        P("head"),
        P("dp"),
        P("dp"),
    )
    out_specs = (P(("dp", "ctx"), "head"), P("dp", "head"))
    return jax.shard_map(shards, mesh=mesh, in_specs=in_specs, out_specs=out_specs, check_vma=False)
```

profile of v0, /device:TPU:1, one launch (start us, length us, event | category | flops | bytes accessed | tf_op | source)
XLA Modules:
  0.0 666.5 jit_solution(2185748450397615939)
XLA Ops:
  10.9 1.3 gather_fusion
  12.6 142.0 %all-gather.6.cloned.1.call-done = bf16[8192,1024]{1,0:T(8,128)(2,1)} async-done(((bf16[256,1024]{1,0:T(8,128)(2,1)}), bf16[8192,1024]{1,0:T(8,128)(2,1)}) %all-gather.6.cloned.1.call-update) | async-done | bytes 16777232 | tf_op jit(solution)/shard_map/all_gather | solution.py:28
  154.6 9.5 %gather_fusion.1 = bf16[256,1024]{1,0:T(8,128)(2,1)S(1)} fusion(bf16[8192,1024]{1,0:T(8,128)(2,1)} %all-gather.6.cloned.1.call-done, s32[1024]{0:T(1024)S(1)} %pad_clamp_fusion.1), kind=kCustom, calls=%fused_computation.1 | custom fusion | bytes 1049600 | tf_op jit(solution)/shard_map/jit(_take)/gather | solution.py:31
  164.7 69.2 %all-gather.4.cloned.1.call-done = bf16[8192,256]{1,0:T(8,128)(2,1)} async-done(((bf16[256,256]{1,0:T(8,128)(2,1)}), bf16[8192,256]{1,0:T(8,128)(2,1)}) %all-gather.4.cloned.1.call-update) | async-done | bytes 4194320 | tf_op jit(solution)/shard_map/all_gather | solution.py:64
  233.9 81.7 %all-gather.8.cloned.1.call-done = bf16[8192,256]{1,0:T(8,128)(2,1)} async-done(((bf16[256,256]{1,0:T(8,128)(2,1)}), bf16[8192,256]{1,0:T(8,128)(2,1)}) %all-gather.8.cloned.1.call-update) | async-done | bytes 4194320 | tf_op jit(solution)/shard_map/all_gather | solution.py:65
  315.6 180.4 %while.15 = (s32[]{:T(128)}, f32[256,2,4]{0,2,1:T(4,128)S(1)}, f32[256,2,4]{0,2,1:T(4,128)S(1)}, f32[256,2,4,128]{0,3,2,1:T(8,128)S(1)}, s32[16,512]{1,0:T(8,128...) while((s32[]{:T(128)}, f32[256,2,4]{0,2,1:T(4,128)S(1)}, ...), condition=%wide.region_3.4_spmd.clone, body=%wide.region_0.3_spmd.clone.sunk | while | flops 551430144 | bytes 18489480 | solution.py:74
  315.9 1.1 constant_dynamic-slice_fusion.6
  317.1 2.8 fusion.57
  319.9 3.2 fusion.58
  323.3 3.6 fusion.60
  328.4 2.8 fusion.57
  331.2 3.2 fusion.58
  334.5 3.6 fusion.60
  338.4 1.1 constant_dynamic-slice_fusion.6
  339.6 2.8 fusion.57
  342.4 3.2 fusion.58
  345.8 3.6 fusion.60
  350.9 2.8 fusion.57
  353.7 3.2 fusion.58
  357.1 3.6 fusion.60
  361.0 1.1 constant_dynamic-slice_fusion.6
  362.2 2.8 fusion.57
  365.0 3.2 fusion.58
  368.4 3.6 fusion.60
  373.5 2.8 fusion.57
  376.3 3.2 fusion.58
  379.6 3.6 fusion.60
  383.5 1.1 constant_dynamic-slice_fusion.6
  384.7 2.8 fusion.57
  387.5 3.2 fusion.58
  390.9 3.6 fusion.60
  394.8 1.1 constant_dynamic-slice_fusion.6
  396.0 2.8 fusion.57
  398.8 3.2 fusion.58
  402.2 3.6 fusion.60
  407.3 2.8 fusion.57
  410.1 3.2 fusion.58
  413.5 3.6 fusion.60
  418.6 2.8 fusion.57
  421.4 3.2 fusion.58
  424.7 3.6 fusion.60
  429.8 2.8 fusion.57
  432.6 3.2 fusion.58
  436.0 3.6 fusion.60
  441.1 2.8 fusion.57
  443.9 3.2 fusion.58
  447.3 3.6 fusion.60
  452.4 2.8 fusion.57
  455.2 3.2 fusion.58
  458.6 3.6 fusion.60
  463.7 2.8 fusion.57
  466.5 3.2 fusion.58
  469.9 3.6 fusion.60
  474.9 2.8 fusion.57
  477.8 3.2 fusion.58
  481.1 3.6 fusion.60
  486.2 2.8 fusion.57
  489.0 3.2 fusion.58
  492.4 3.6 fusion.60
  496.5 10.0 %psum.21 = f32[256]{0:T(256)S(1)} all-reduce(f32[256]{0:T(256)S(1)} %get-tuple-element.123), channel_id=1, replica_groups=mesh['dp'=2,'ctx'=32,'head'=4] {'head'}, use_global_device_ids=true, to_apply=%region_5.6 | all-reduce | flops 256 | bytes 2048 | tf_op jit(solution)/shard_map/psum | solution.py:87
  506.7 1.5 fusion.41
  508.1 1.5 fusion.40
  511.3 112.7 %psum.22 = bf16[16,1024]{1,0:T(8,128)(2,1)S(1)} all-reduce(bf16[16,1024]{1,0:T(8,128)(2,1)S(1)} %convolution_convert_fusion), channel_id=1, replica_groups=mesh['dp'=2,'ctx'=32,'head'=4] {'ctx'}, use_global_device_ids=true, to_apply=%region_10.11 | all-reduce | flops 16384 | bytes 65536 | tf_op jit(solution)/shard_map/psum | solution.py:117
  624.1 35.2 %psum.23 = f32[16]{0:T(128)S(1)} all-reduce(f32[16]{0:T(128)S(1)} %fusion.36), channel_id=1, replica_groups=mesh['dp'=2,'ctx'=32,'head'=4] {'head'}, use_global_device_ids=true, to_apply=%region_12.13 | all-reduce | flops 16 | bytes 128 | tf_op jit(solution)/shard_map/psum | solution.py:119
  (180 shorter events, 28.1 us)
Async XLA Ops:
  7.2 147.5 %all-gather.6.cloned.1.call-start = ((), (), s32[]{:S(2)}) async-start(), calls=%async_computation.1 | async-start | bytes 17301504 | tf_op jit(solution)/shard_map/all_gather | solution.py:28
  7.9 226.0 %all-gather.4.cloned.1.call-start = ((), (), s32[]{:S(2)}) async-start(), calls=%async_computation | async-start | bytes 4325376 | tf_op jit(solution)/shard_map/all_gather | solution.py:64
  8.6 307.0 %all-gather.8.cloned.1.call-start = ((), (), s32[]{:S(2)}) async-start(), calls=%async_computation.2 | async-start | bytes 4325376 | tf_op jit(solution)/shard_map/all_gather | solution.py:65
  315.6 190.8 %copy-start.1 = (f32[1024]{0:T(1024)S(1)}, f32[1024]{0:T(1024)}, u32[]{:S(2)}) copy-start(f32[1024]{0:T(1024)} %param.13) | copy-start | bytes 12292
  496.5 14.4 %copy-start = (bf16[256,1024]{1,0:T(8,128)(2,1)}, bf16[256,1024]{1,0:T(8,128)(2,1)S(1)}, u32[]{:S(2)}) copy-start(bf16[256,1024]{1,0:T(8,128)(2,1)S(1)} %copy.26) | copy-start | bytes 1572868
  496.5 13.3 %copy-start.2 = (bf16[512,1024]{1,0:T(8,128)(2,1)S(1)}, bf16[512,1024]{1,0:T(8,128)(2,1)}, u32[]{:S(2)}) copy-start(bf16[512,1024]{1,0:T(8,128)(2,1)} %param.12) | copy-start | bytes 3145732
Sparse Core Ops, SparseCore 0:
  10.6 144.0 all-gather.5
  157.2 76.6 all-gather.3
  236.5 79.0 all-gather.7
where the time goes:
time: 668 us; the launch traced here: 666 us
  waiting for transfers between devices  295 us (44%)
  blocking collectives  158 us (24%)
  matrix products  107 us (16%)
  other arithmetic  56.9 us (9%)
  local copies, waits for them, and re-layouts  35.2 us (5%)
  between operations  13.9 us (2%)
    all_gather x1, waiting for transfers between devices, shards(): piece = lax.all_gather(queries, 'ctx', axis=0, tiled=True)  142 us
    psum x1, blocking collectives, shards(): lax.psum(local_sums.astype(jnp.bfloat16), 'ctx').astype(jnp.float32)  113 us
    all_gather x1, waiting for transfers between devices, shards(): value_piece = lax.all_gather(values, 'ctx', axis=0, tiled=True)  81.7 us
    all_gather x1, waiting for transfers between devices, shards(): key_piece = lax.all_gather(keys, 'ctx', axis=0, tiled=True)  69.2 us
    dot_general x16, matrix products, add_tile(): jnp.einsum('nkgm,mkd->nkgd', weights.astype(jnp.bfloat16), value_heads, p...  57.5 us
    reduce_sum x16, other arithmetic, add_tile(): running_sum = running_sum * rescale + jnp.sum(weights, axis=-1)  51.3 us
    dot_general x16, matrix products, add_tile(): jnp.einsum('nkgd,mkd->nkgm', query_heads, key_heads, preferred_element_ty...  44.8 us
    psum x1, blocking collectives, shards(): doc_total = lax.psum(doc_squares, 'head')  35.2 us
  transfers between devices with their start and end apart: 3, of which 3 were waited for; matrix products, arithmetic and copies ran while one was open for 2% of the time, Pallas kernels for 0%

commit v1 on v0

v1 whole, which is shorter than its diff:
```python
import math

import jax
import jax.numpy as jnp
from jax import lax
from jax.experimental import pallas as pl
from jax.experimental.pallas import tpu as pltpu
from jax.sharding import PartitionSpec as P

HEADS = 32
HEAD_DIM = 128
BLOCK = 128
BLOCKS = 64
LONG = 40
DOCS = 16
CHANNELS = HEADS * HEAD_DIM
PIECE = 8
ROWS = 4 * PIECE
TILE = 256
CHUNK = 1024
LONG_KEYS = LONG * BLOCK
SHORT_KEYS = (BLOCKS - LONG) * BLOCK
EPS = 1e-05
MESH = pl.DeviceIdType.MESH
F32 = jnp.float32
BF16 = jnp.bfloat16


def loop(count, body):
    def step(i, carry):
        body(i)
        return carry

    lax.fori_loop(0, count, step, 0)


class Place:
    def __init__(self):
        self.ctx = lax.axis_index("ctx")
        head = lax.axis_index("head")
        self.z = self.ctx // 4
        self.y = self.ctx % 4
        self.plane = head // 2
        self.core = head % 2
        self.kv = self.z % 4
        self.piece = (self.z // 4) * 8 + self.y * 2 + self.core

    def at(self, z, y, core, plane=None):
        plane = self.plane if plane is None else plane
        return {"ctx": z * 4 + y, "head": plane * 2 + core}

    def worker(self, kv, piece):
        return (kv + 4 * (piece // 8), (piece % 8) // 2, piece % 2)

    def is_me(self, z, y, core):
        return (z == self.z) & (y == self.y) & (core == self.core)


def enter(me, others=0):
    barrier = pltpu.get_barrier_semaphore()

    def greet(i):
        z, y, core = i // 8, (i // 2) % 4, i % 2

        @pl.when(jnp.logical_not(me.is_me(z, y, core)))
        def _():
            pl.semaphore_signal(barrier, 1, device_id=me.at(z, y, core), device_id_type=MESH)

    loop(64, greet)
    if others:

        def greet_other(kv):
            pl.semaphore_signal(
                barrier,
                1,
                device_id=me.at(kv + 4 * (me.z // 4), me.y, me.core, 1 - me.plane),
                device_id_type=MESH,
            )

        loop(4, greet_other)
    pl.semaphore_wait(barrier, 63 + others)


def send(src, dst, send_sem, recv_sem, device):
    return pltpu.make_async_remote_copy(
        src_ref=src, dst_ref=dst, send_sem=send_sem, recv_sem=recv_sem, device_id=device, device_id_type=MESH
    )


def arrived(ref, sem):
    pltpu.make_async_copy(ref, ref, sem).wait()


def spread_kernel(
    q_ref, k_ref, v_ref, lat_ref, gain_ref,
    qp_ref, kv_ref, lat_out, gain_out,
    qs, s_a, r_a, s_b, r_b, s_c, r_c, s_s, r_s, s_q, r_q, s_l, r_l,
):
    me = Place()
    z, y, core = me.z, me.y, me.core
    enter(me)
    up, down = (y + 1) % 4, (y + 3) % 4
    mine = me.kv // 2 == core

    def column(run):
        for half in range(2):
            for far in range(2):
                for kind in range(2):
                    to_z = 2 * core + half + 4 * far
                    slot = half * 4 + far * 2 + kind
                    src = (k_ref, v_ref)[kind].at[:, pl.ds(half * HEAD_DIM, HEAD_DIM)]
                    dst = kv_ref.at[kind, pl.ds(me.ctx * 256, 256), :]
                    here = (to_z == z) & (core == kind)
                    copy = send(src, dst, s_a.at[slot], r_a.at[z], me.at(to_z, y, kind))
                    run(here, copy, src, dst)

    def start_column(here, copy, src, dst):
        @pl.when(here)
        def _():
            pltpu.make_async_copy(src, dst, r_a.at[z]).start()

        @pl.when(jnp.logical_not(here))
        def _():
            copy.start()

    def end_column(here, copy, src, dst):
        @pl.when(jnp.logical_not(here))
        def _():
            copy.wait_send()

    column(start_column)

    def pool_inputs():
        other = me.at(z, y, 1 - core)
        half = me.kv % 2
        lat = lat_ref.at[:, pl.ds(pl.multiple_of(half * 512, 512), 512)]
        gain = gain_ref.at[half]
        return (
            pltpu.make_async_copy(lat, lat_out, r_l.at[0]),
            pltpu.make_async_copy(gain, gain_out, r_l.at[1]),
            send(lat, lat_out, s_l.at[0], r_l.at[0], other),
            send(gain, gain_out, s_l.at[1], r_l.at[1], other),
        )

    @pl.when(mine)
    def _():
        for copy in pool_inputs():
            copy.start()

    for half in range(2):
        for block in range(2):
            for pair in range(8):
                tile = q_ref[block * BLOCK + pair * 16 : block * BLOCK + pair * 16 + 16, half * 512 : half * 512 + 512]
                tile = tile.astype(F32)
                for part in range(2):
                    rows = tile[part * 8 : part * 8 + 8]
                    rows = jnp.concatenate([rows[:, h * 128 : h * 128 + 128] for h in range(4)], axis=0)
                    qs[half * 16 + pair * 2 + part, block * ROWS : block * ROWS + ROWS, :] = rows.astype(BF16)

    def query(j, run):
        i = (j + me.ctx) % 32
        to = me.worker(2 * core + i // 16, i % 16)
        run(
            me.is_me(*to),
            send(qs.at[i], qp_ref.at[me.ctx], s_q.at[i], r_q.at[me.ctx], me.at(*to)),
            pltpu.make_async_copy(qs.at[i], qp_ref.at[me.ctx], r_q.at[me.ctx]),
        )

    def start_query(here, remote, local):
        @pl.when(here)
        def _():
            local.start()

        @pl.when(jnp.logical_not(here))
        def _():
            remote.start()

    def end_query(here, remote, local):
        @pl.when(jnp.logical_not(here))
        def _():
            remote.wait_send()

    loop(32, lambda j: query(j, start_query))

    def rows_of(from_z, from_y, first=0, count=256):
        start = pl.multiple_of((from_z * 4 + from_y) * 256 + first, 128)
        return kv_ref.at[core, pl.ds(start, count), :]

    def to_core(from_z, from_y):
        s = from_z * 4 + from_y
        rows = rows_of(from_z, from_y)
        return send(rows, rows, s_s.at[s], r_s.at[s], me.at(z, y, 1 - core))

    def near(from_z):
        rows = rows_of(from_z, y)
        return (
            send(rows, rows, s_b.at[0, from_z], r_b.at[0, from_z], me.at(z, up, core)),
            send(rows, rows, s_b.at[1, from_z], r_b.at[1, from_z], me.at(z, down, core)),
            to_core(from_z, y),
        )

    def onward(from_z):
        one = rows_of(from_z, down, 0, 128)
        two = rows_of(from_z, up, 128, 128)
        return (
            send(one, one, s_c.at[0, from_z], r_c.at[0, from_z], me.at(z, up, core)),
            to_core(from_z, down),
            send(two, two, s_c.at[1, from_z], r_c.at[1, from_z], me.at(z, down, core)),
            to_core(from_z, up),
        )

    def order(j):
        odd = j % 2
        return (z + odd * ((j + 1) // 2) + (1 - odd) * (8 - j // 2)) % 8

    def ring(j):
        @pl.when(j < 8)
        def _():
            from_z = order(j)
            arrived(rows_of(from_z, y), r_a.at[from_z])
            for copy in near(from_z):
                copy.start()

        @pl.when((j >= 2) & (j < 10))
        def _():
            from_z = order(j - 2)
            copies = onward(from_z)
            arrived(rows_of(from_z, down), r_b.at[0, from_z])
            copies[0].start()
            copies[1].start()
            arrived(rows_of(from_z, up), r_b.at[1, from_z])
            copies[2].start()
            copies[3].start()

        @pl.when(j >= 4)
        def _():
            from_z = order(j - 4)
            opposite = (y + 2) % 4
            arrived(rows_of(from_z, opposite, 0, 128), r_c.at[0, from_z])
            arrived(rows_of(from_z, opposite, 128, 128), r_c.at[1, from_z])
            to_core(from_z, opposite).start()

    loop(12, ring)

    def finish_ring(from_z):
        for copy in near(from_z) + onward(from_z) + (to_core(from_z, (y + 2) % 4),):
            copy.wait_send()

    column(end_column)
    loop(8, finish_ring)
    loop(32, lambda j: query(j, end_query))

    def finish(s):
        arrived(qp_ref.at[s], r_q.at[s])
        arrived(kv_ref.at[1 - core, pl.ds(pl.multiple_of(s * 256, 256), 256), :], r_s.at[s])

    loop(32, finish)
    for copy in pool_inputs()[:2]:
        copy.wait()

    @pl.when(mine)
    def _():
        for copy in pool_inputs()[2:]:
            copy.wait_send()


def spread(queries, keys, values, latents, gain):
    dma = pltpu.SemaphoreType.DMA
    hbm = pl.BlockSpec(memory_space=pl.ANY)
    vmem = pl.BlockSpec(memory_space=pltpu.VMEM)
    return pl.pallas_call(
        spread_kernel,
        out_shape=(
            jax.ShapeDtypeStruct((32, 2 * ROWS, HEAD_DIM), BF16),
            jax.ShapeDtypeStruct((2, BLOCKS * BLOCK, HEAD_DIM), BF16),
            jax.ShapeDtypeStruct((512, 512), BF16),
            jax.ShapeDtypeStruct((4, 128), F32),
        ),
        in_specs=[vmem, hbm, hbm, hbm, hbm],
        out_specs=(hbm, hbm, hbm, hbm),
        scratch_shapes=[
            pltpu.VMEM((32, 2 * ROWS, HEAD_DIM), BF16),
            dma((8,)), dma((8,)),
            dma((2, 8)), dma((2, 8)),
            dma((2, 8)), dma((2, 8)),
            dma((32,)), dma((32,)),
            dma((32,)), dma((32,)),
            dma((2,)), dma((2,)),
        ],
        compiler_params=pltpu.CompilerParams(
            collective_id=0, has_side_effects=True, vmem_limit_bytes=32 * 1024 * 1024
        ),
        name="spread",
    )(queries, keys, values, latents, gain)


def attend_kernel(doc_ref, source_ref, q_ref, kv_ref, out_ref, sq_ref, hot_ref, ka, va, qa, scores, peak, o_ref):
    first = lax.fori_loop(
        0,
        BLOCKS - LONG + 1,
        lambda i, found: jnp.where(doc_ref[i] == doc_ref[i + LONG - 1], i, found),
        jnp.int32(0),
    )

    def packed(i):
        return jnp.where(i < LONG, first + i, jnp.where(i - LONG < first, i - LONG, i))

    scale = math.log2(math.e) * HEAD_DIM ** (-0.5)

    def arrange(i):
        at = packed(i)
        here = pl.ds(pl.multiple_of(i * BLOCK, BLOCK), BLOCK)
        there = pl.ds(pl.multiple_of(at * BLOCK, BLOCK), BLOCK)
        key = kv_ref[0, there, :]
        ka[here, 0:128] = key
        ka[here, 128:256] = key
        va[here, 0:128] = kv_ref[1, there, :]
        va[here, 128:256] = jnp.ones((BLOCK, 128), BF16)
        query = q_ref[pl.ds(pl.multiple_of(at * ROWS, ROWS), ROWS), :].astype(F32) * scale
        high = query.astype(BF16)
        rows = pl.ds(pl.multiple_of(i * ROWS, ROWS), ROWS)
        qa[rows, 0:128] = high
        qa[rows, 128:256] = (query - high.astype(F32)).astype(BF16)

    loop(BLOCKS, arrange)

    def tile_rows(t):
        return pl.ds(pl.multiple_of(t * TILE, TILE), TILE)

    def score_chunk(t, slot, c, base, top, docs=None):
        q = qa[tile_rows(t), :]
        k = ka[base + c * CHUNK : base + (c + 1) * CHUNK, :]
        s = lax.dot_general(q, k, (((1,), (1,)), ((), ())), preferred_element_type=F32)
        if docs is not None:
            parts = []
            for b in range(CHUNK // BLOCK):
                key_doc = doc_ref[packed(jnp.int32((base + c * CHUNK) // BLOCK + b))]
                parts.append(jnp.where(docs == key_doc, s[:, b * 128 : b * 128 + 128], -1e30))
            s = jnp.concatenate(parts, axis=1)
        scores[slot, :, c * CHUNK : (c + 1) * CHUNK] = s
        for b in range(CHUNK // 128):
            part = s[:, b * 128 : b * 128 + 128]
            top = part if top is None else jnp.maximum(top, part)
        return top

    def close_scores(slot, top):
        peak[slot] = jnp.broadcast_to(jnp.max(top, axis=1, keepdims=True), (TILE, 128))

    def mix_chunk(slot, c, base, total):
        m = peak[slot]
        parts = []
        for b in range(CHUNK // 128):
            s = scores[slot, :, c * CHUNK + b * 128 : c * CHUNK + b * 128 + 128]
            parts.append(jnp.exp2(s - m).astype(BF16))
        w = jnp.concatenate(parts, axis=1)
        v = va[base + c * CHUNK : base + (c + 1) * CHUNK, :]
        add = jnp.dot(w, v, preferred_element_type=F32)
        return add if total is None else total + add

    def close_mix(t, total):
        o_ref[tile_rows(t), :] = (total[:, 0:128] / total[:, 128:256]).astype(BF16)

    long_tiles = LONG * ROWS // TILE
    long_chunks = LONG_KEYS // CHUNK
    short_tiles = (BLOCKS - LONG) * ROWS // TILE
    short_chunks = SHORT_KEYS // CHUNK

    top = None
    for c in range(long_chunks):
        top = score_chunk(0, 0, c, 0, top)
    close_scores(0, top)

    def step(t):
        slot = t % 2
        top, total = None, None
        for c in range(long_chunks):
            top = score_chunk(t + 1, 1 - slot, c, 0, top)
            total = mix_chunk(slot, c, 0, total)
        close_scores(1 - slot, top)
        close_mix(t, total)

    loop(long_tiles - 1, step)

    def row_docs(t):
        per = TILE // ROWS
        return jnp.concatenate(
            [jnp.full((ROWS, 128), doc_ref[packed(t * per + b)], jnp.int32) for b in range(per)], axis=0
        )

    def short_step(i):
        t = long_tiles + i
        slot = t % 2
        docs = row_docs(t)
        top, total = None, None
        for c in range(short_chunks):
            top = score_chunk(t, slot, c, LONG_KEYS, top, docs)
        close_scores(slot, top)
        for c in range(short_chunks):
            total = mix_chunk(slot, c, LONG_KEYS, total)
        close_mix(t, total)

    last = long_tiles - 1
    total = None
    for c in range(long_chunks):
        total = mix_chunk(last % 2, c, 0, total)
    close_mix(last, total)
    loop(short_tiles, short_step)

    lanes = lax.broadcasted_iota(jnp.int32, (PIECE, 128), 1)

    def squares(half):
        part = peak[0]
        high = part.astype(BF16)
        low = (part - high.astype(F32)).astype(BF16)
        ones = jnp.ones((8, 128), BF16)
        dims = (((1,), (1,)), ((), ()))
        sq_ref[:, half * 256 : half * 256 + 256] = lax.dot_general(
            ones, high, dims, preferred_element_type=F32
        ) + lax.dot_general(ones, low, dims, preferred_element_type=F32)
        hot_ref[:, half * 256 : half * 256 + 256] = jnp.transpose(scores[0, :, 0:128])[0:DOCS].astype(BF16)

    for half in range(2):
        def move_half(i, half=half):
            p = half * 32 + i
            at = source_ref[p]
            doc = doc_ref[at]
            row = jnp.where(at < first, at + LONG, jnp.where(at < first + LONG, at - first, at))
            piece = o_ref[pl.ds(pl.multiple_of(row * ROWS, ROWS), ROWS), :]
            out_ref[p] = piece
            wide = piece.astype(F32)
            wide = wide * wide
            here = pl.ds(pl.multiple_of(i * PIECE, PIECE), PIECE)
            peak[0, here, :] = wide[0:8] + wide[8:16] + wide[16:24] + wide[24:32]
            scores[0, here, 0:128] = (lanes == doc).astype(F32)

        loop(32, move_half)
        squares(half)


def attend(block_doc, block_source, q, kv):
    smem = pl.BlockSpec(memory_space=pltpu.SMEM)
    vmem = pl.BlockSpec(memory_space=pltpu.VMEM)
    return pl.pallas_call(
        attend_kernel,
        out_shape=(
            jax.ShapeDtypeStruct((BLOCKS, ROWS, HEAD_DIM), BF16),
            jax.ShapeDtypeStruct((8, BLOCKS * PIECE), F32),
            jax.ShapeDtypeStruct((DOCS, BLOCKS * PIECE), BF16),
        ),
        in_specs=[smem, smem, vmem, vmem],
        out_specs=(vmem, vmem, vmem),
        scratch_shapes=[
            pltpu.VMEM((BLOCKS * BLOCK, 256), BF16),
            pltpu.VMEM((BLOCKS * BLOCK, 256), BF16),
            pltpu.VMEM((BLOCKS * ROWS, 256), BF16),
            pltpu.VMEM((2, TILE, LONG_KEYS), F32),
            pltpu.VMEM((2, TILE, 128), F32),
            pltpu.VMEM((BLOCKS * ROWS, HEAD_DIM), BF16),
        ],
        compiler_params=pltpu.CompilerParams(vmem_limit_bytes=48 * 1024 * 1024),
        name="attend",
    )(block_doc, block_source, q, kv)


def collect_kernel(
    o_ref, sq_ref, hot_ref, lat_ref, gain_ref,
    att_ref, emb_ref,
    home, sq_in, doc_out, doc_in, norm_out, norm_in, row_out, row_in,
    s_o, r_o, s_sq, r_sq, s_d, r_d, s_n, r_n, s_e, r_e,
):
    me = Place()
    enter(me, 4)
    me8 = me.plane * 4 + me.kv
    to_core = me.kv // 2
    half = me.kv % 2

    def partners(src, box, s_sem, r_sem, run):
        def one(i):
            @pl.when(i != me8)
            def _():
                device = me.at(i % 4 + 4 * (me.z // 4), me.y, me.core, i // 4)
                run(send(src, box.at[me8], s_sem.at[i], r_sem.at[me8], device))

        loop(8, one)

    def from_partners(box, r_sem):
        def one(i):
            @pl.when(i != me8)
            def _():
                arrived(box.at[i], r_sem.at[i])

        loop(8, one)

    start = lambda copy: copy.start()
    sent = lambda copy: copy.wait_send()

    partners(sq_ref, sq_in, s_sq, r_sq, start)
    sq_in[me8] = sq_ref[...]

    def result(j, run):
        s = (j + me.ctx) % 32
        src = o_ref.at[pl.ds(2 * s, 2)]
        slot = half * 16 + me.piece
        run(
            me.is_me(s // 4, s % 4, to_core),
            send(src, home.at[slot], s_o.at[s], r_o.at[slot], me.at(s // 4, s % 4, to_core)),
            pltpu.make_async_copy(src, home.at[slot], r_o.at[slot]),
        )

    def start_either(here, remote, local):
        @pl.when(here)
        def _():
            local.start()

        @pl.when(jnp.logical_not(here))
        def _():
            remote.start()

    def end_either(here, remote, local):
        @pl.when(jnp.logical_not(here))
        def _():
            remote.wait_send()

    loop(32, lambda j: result(j, start_either))

    from_partners(sq_in, r_sq)
    channel_total = jnp.sum(sq_in[...], axis=0)[0:1]
    factor = lax.rsqrt(channel_total / CHANNELS + EPS)
    factor = jnp.transpose(jnp.broadcast_to(factor, (128, BLOCKS * PIECE)))
    whole = o_ref[...].astype(F32).reshape(BLOCKS, 4, PIECE, 128)
    normed = []
    for h in range(4):
        part = whole[:, h].reshape(BLOCKS * PIECE, 128)
        normed.append((part * factor * gain_ref[h : h + 1, :]).astype(BF16))
    normed = jnp.concatenate(normed, axis=1)

    lat = lat_ref[...]
    s = lax.dot_general(normed, lat, (((1,), (1,)), ((), ())), preferred_element_type=F32) * 512 ** (-0.5)
    w = jnp.exp(s - jnp.max(s, axis=-1, keepdims=True))
    w = (w / jnp.sum(w, axis=-1, keepdims=True)).astype(BF16)
    by_doc = jnp.dot(hot_ref[...], w, preferred_element_type=F32)
    sums = None
    for _ in range(3):
        part = by_doc.astype(BF16)
        by_doc = by_doc - part.astype(F32)
        add = jnp.dot(part, lat, preferred_element_type=F32)
        sums = add if sums is None else sums + add

    doc_out[...] = jnp.zeros_like(doc_out)
    for h in range(4):
        doc_out[:, h, :] = sums[:, h * 128 : h * 128 + 128]

    def document(d, run):
        to = me.worker(me.kv, d)
        run(
            d == me.piece,
            send(doc_out.at[d], doc_in.at[me.piece], s_d.at[d], r_d.at[me.piece], me.at(*to)),
            pltpu.make_async_copy(doc_out.at[d], doc_in.at[me.piece], r_d.at[me.piece]),
        )

    loop(DOCS, lambda d: document(d, start_either))
    loop(DOCS, lambda d: arrived(doc_in.at[d], r_d.at[d]))
    total = jnp.sum(doc_in[...], axis=0)
    norm_out[...] = jnp.broadcast_to(jnp.sum(total * total, keepdims=True), (8, 128))
    partners(norm_out, norm_in, s_n, r_n, start)
    norm_in[me8] = norm_out[...]
    from_partners(norm_in, r_n)
    doc_total = jnp.sum(norm_in[...], axis=0)
    row_out[...] = total * lax.rsqrt(doc_total / CHANNELS + EPS)

    def share(j, run):
        s = (j + me.ctx) % 32
        dst = row_in.at[half, me.piece]
        slot = half * 16 + me.piece
        run(
            me.is_me(s // 4, s % 4, to_core),
            send(row_out, dst, s_e.at[s], r_e.at[slot], me.at(s // 4, s % 4, to_core)),
            pltpu.make_async_copy(row_out, dst, r_e.at[slot]),
        )

    loop(32, lambda j: share(j, start_either))

    loop(32, lambda i: arrived(home.at[i], r_o.at[i]))
    for side in range(2):
        for block in range(2):
            for pair in range(8):
                rows = []
                for part in range(2):
                    piece = home[side * 16 + pair * 2 + part, block].astype(F32)
                    rows.append(jnp.concatenate([piece[h * 8 : h * 8 + 8] for h in range(4)], axis=1))
                at = block * BLOCK + pair * 16
                att_ref[at : at + 16, side * 512 : side * 512 + 512] = jnp.concatenate(rows, axis=0).astype(BF16)

    loop(32, lambda i: arrived(row_in.at[i // 16, i % 16], r_e.at[i]))
    for side in range(2):
        for h in range(4):
            at = side * 512 + h * 128
            emb_ref[:, at : at + 128] = row_in[side, :, h, :]

    partners(sq_ref, sq_in, s_sq, r_sq, sent)
    partners(norm_out, norm_in, s_n, r_n, sent)
    loop(32, lambda j: result(j, end_either))
    loop(DOCS, lambda d: document(d, end_either))
    loop(32, lambda j: share(j, end_either))


def collect(results, squares, hot, latents, gain):
    dma = pltpu.SemaphoreType.DMA
    vmem = pl.BlockSpec(memory_space=pltpu.VMEM)
    return pl.pallas_call(
        collect_kernel,
        out_shape=(
            jax.ShapeDtypeStruct((256, 1024), BF16),
            jax.ShapeDtypeStruct((DOCS, 1024), F32),
        ),
        in_specs=[vmem] * 5,
        out_specs=(vmem, vmem),
        scratch_shapes=[
            pltpu.VMEM((32, 2, ROWS, HEAD_DIM), BF16),
            pltpu.VMEM((8, 8, BLOCKS * PIECE), F32),
            pltpu.VMEM((DOCS, 8, 128), F32),
            pltpu.VMEM((DOCS, 8, 128), F32),
            pltpu.VMEM((8, 128), F32),
            pltpu.VMEM((8, 8, 128), F32),
            pltpu.VMEM((8, 128), F32),
            pltpu.VMEM((2, DOCS, 8, 128), F32),
            dma((32,)), dma((32,)),
            dma((8,)), dma((8,)),
            dma((DOCS,)), dma((DOCS,)),
            dma((8,)), dma((8,)),
            dma((32,)), dma((32,)),
        ],
        compiler_params=pltpu.CompilerParams(
            collective_id=1, has_side_effects=True, vmem_limit_bytes=40 * 1024 * 1024
        ),
        name="collect",
    )(results, squares, hot, latents, gain)


def shards(queries, keys, values, latents, norm_gain, block_doc, block_source):
    q, kv, lat, gain = spread(queries, keys, values, latents, norm_gain.reshape(2, 4, 128))
    results, squares, hot = attend(block_doc, block_source, q.reshape(BLOCKS * ROWS, HEAD_DIM), kv)
    return collect(results, squares, hot, lat, gain)


def solution(mesh):
    in_specs = (
        P(("dp", "ctx"), "head"),
        P(("dp", "ctx"), "head"),
        P(("dp", "ctx"), "head"),
        P(None, "head"),
        P("head"),
        P("dp"),
        P("dp"),
    )
    out_specs = (P(("dp", "ctx"), "head"), P("dp", "head"))
    return jax.shard_map(shards, mesh=mesh, in_specs=in_specs, out_specs=out_specs, check_vma=False)
```

time: 668 us -> 124 us (0.19)
  waiting for transfers between devices: 295 us -> 0 us
  blocking collectives: 158 us -> 0 us
  Pallas kernels: 0 us -> 116 us
  matrix products: 107 us -> 0 us
  other arithmetic: 56.9 us -> 0 us
  local copies, waits for them, and re-layouts: 35.2 us -> 7.48 us
  between operations: 13.9 us -> 0.67 us
    all_gather x3 -> x0, waiting for transfers between devices: 293 us -> none  [the longest x1 142 us: shards(): piece = lax.all_gather(queries, 'ctx', axis=0, tiled=True)]
    psum x3 -> x0, blocking collectives: 158 us -> none  [the longest x1 113 us: shards(): lax.psum(local_sums.astype(jnp.bfloat16), 'ctx').astype(jnp.float32)]
    pallas_call x0 -> x3, Pallas kernels: none -> 116 us  [the longest x1 47.4 us: spread(): pl.pallas_call(spread_kernel, out_shape=(jax.ShapeDtypeStruct((32, 2 * RO...]
    dot_general x37 -> x0, matrix products: 107 us -> none  [the longest x16 57.5 us: add_tile(): jnp.einsum('nkgm,mkd->nkgd', weights.astype(jnp.bfloat16), value_heads, p...]
    reduce_sum x20 -> x0, other arithmetic: 52.1 us -> none  [the longest x16 51.3 us: add_tile(): running_sum = running_sum * rescale + jnp.sum(weights, axis=-1)]
    dynamic_slice x64 -> x0, local copies, waits for them, and re-layouts: 21.8 us -> none  [shards(): lax.scan(scan_step, initial, (key_piece.reshape(tile_count, tile_rows, -1...]
    gather x3 -> x0, local copies, waits for them, and re-layouts: 11.1 us -> none  [the longest x2 9.85 us: shards(): taken = jnp.take(piece, jnp.clip(source_rows, 0, piece_rows - 1), axis=0)]
    unnamed x7 -> x16, local copies, waits for them, and re-layouts: 0.02 us -> 7.48 us
  transfers between devices with their start and end apart: 3 -> 0, of which waited for: 3 -> 0; matrix products, arithmetic and copies ran while one was open for 2% -> 0% of each run, Pallas kernels for 0% -> 0%
where the time goes in v1:
time: 124 us
  Pallas kernels  116 us (94%)
  local copies, waits for them, and re-layouts  7.48 us (6%)
    pallas_call x1, Pallas kernels, spread(): pl.pallas_call(spread_kernel, out_shape=(jax.ShapeDtypeStruct((32, 2 * RO...  47.4 us
    pallas_call x1, Pallas kernels, collect(): pl.pallas_call(collect_kernel, out_shape=(jax.ShapeDtypeStruct((256, 1024...  43.6 us
    pallas_call x1, Pallas kernels, attend(): pl.pallas_call(attend_kernel, out_shape=(jax.ShapeDtypeStruct((BLOCKS, RO...  24.8 us
    unnamed x16, local copies, waits for them, and re-layouts  7.48 us

profile of v1, /device:TPU:1, one launch (start us, length us, event | category | flops | bytes accessed | tf_op | source)
XLA Modules:
  0.0 124.0 jit_solution(5413363381546908332)
XLA Ops:
  0.6 0.0 copy-start
  0.6 1.2 copy-done
  1.9 0.0 copy-start.1
  1.9 1.0 copy-done.1
  2.9 0.0 copy-start.2
  2.9 0.9 copy-done.2
  3.8 0.0 copy-start.3
  3.8 0.9 copy-done.3
  4.7 0.0 copy-start.4
  4.7 0.7 copy-done.4
  5.4 47.4 %spread.1 = (bf16[32,64,128]{2,1,0:T(8,128)(2,1)S(1)}, bf16[2,8192,128]{2,1,0:T(8,128)(2,1)S(1)}, bf16[512,512]{1,0:T(8,128)(2,1)S(1)}, f32[4,128]{1,0:T(4,128)S(1)}) custom-call(bf16[256,1024]{1,0:T(8,128)(2,1)S(1)} %copy-done.1, bf16[256,256]{1,0:T(8,128)(2,1)S(1)} %copy-done.2, bf16[256,256]{1,0:T(8,128)(2,1)S(1)} %copy-done.3, ...), custom_call_target="tpu_custom_call" | custom-call | tf_op jit(solution)/shard_map/spread/pallas_call | solution.py:271
  52.8 0.0 copy-start.5
  52.8 0.6 copy-done.5
  53.5 0.0 copy-start.6
  53.5 0.7 copy-done.6
  54.1 24.8 %attend.1 = (bf16[64,32,128]{2,1,0:T(8,128)(2,1)S(1)}, f32[8,512]{1,0:T(8,128)S(1)}, bf16[16,512]{1,0:T(8,128)(2,1)S(1)}) custom-call(s32[64]{0:T(128)S(1)} %copy-done.5, s32[64]{0:T(128)S(1)} %copy-done.6, bf16[2048,128]{1,0:T(8,128)(2,1)S(1)} %bitcast.2, bf16[2,8192,128]{2,1,0:T(8,128)(2,1)S(1)} %get-tuple-element.10.kv_ref), custom_call_target="tpu_custom_call" | custom-call | tf_op jit(solution)/shard_map/attend/pallas_call | solution.py:443
  78.9 43.6 %collect.1 = (bf16[256,1024]{1,0:T(8,128)(2,1)S(1)}, f32[16,1024]{1,0:T(8,128)S(1)}) custom-call(bf16[64,32,128]{2,1,0:T(8,128)(2,1)S(1)} %get-tuple-element.11.o_ref, f32[8,512]{1,0:T(8,128)S(1)} %get-tuple-element.12.sq_ref, bf16[16,512]{1,0:T(8,128)(2,1)S(1)} %get-tuple-element.13.hot_ref, bf16[512,512]{1,0:T(8,128)(2,1)S(1)} %get-tuple-element.14.lat_ref, ...), custom_call_target="tpu_custom_call" | custom-call | tf_op jit(solution)/shard_map/collect/pallas_call | solution.py:610
  122.6 0.8 copy.11
  123.4 0.6 copy.12
Async XLA Ops:
  0.6 1.2 copy-start
  1.9 1.0 copy-start.1
  2.9 0.9 copy-start.2
  3.8 0.9 copy-start.3
  4.7 0.7 copy-start.4
  52.8 0.7 copy-start.5
  53.5 0.7 copy-start.6

commit v2 on v1

v2 whole, which is shorter than its diff:
```python
import functools
import math

import jax
import jax.numpy as jnp
from jax import lax
from jax.experimental import pallas as pl
from jax.experimental.pallas import tpu as pltpu
from jax.sharding import PartitionSpec as P

HEADS = 32
HEAD_DIM = 128
BLOCK = 128
BLOCKS = 64
LONG = 40
DOCS = 16
CHANNELS = HEADS * HEAD_DIM
PIECE = 8
ROWS = 4 * PIECE
TILE = 640
SHORT_TILE = 384
CHUNK = 256
LONG_KEYS = LONG * BLOCK
SHORT_KEYS = (BLOCKS - LONG) * BLOCK
EPS = 1e-05
PARTS = 1
PART = 256 // PARTS
HALF = PART // 2
AHEAD = 4
Q_START = 4
Q_STEP = 4
LAG = 4
MESH = pl.DeviceIdType.MESH
F32 = jnp.float32
BF16 = jnp.bfloat16


def loop(count, body):
    def step(i, carry):
        body(i)
        return carry

    lax.fori_loop(0, count, step, 0)


class Place:
    def __init__(self):
        self.ctx = lax.axis_index("ctx")
        head = lax.axis_index("head")
        self.z = self.ctx // 4
        self.y = self.ctx % 4
        self.plane = head // 2
        self.core = head % 2
        self.kv = self.z % 4
        self.piece = (self.z // 4) * 8 + self.y * 2 + self.core

    def at(self, z, y, core, plane=None):
        plane = self.plane if plane is None else plane
        return {"ctx": z * 4 + y, "head": plane * 2 + core}

    def worker(self, kv, piece):
        return (kv + 4 * (piece // 8), (piece % 8) // 2, piece % 2)

    def is_me(self, z, y, core):
        return (z == self.z) & (y == self.y) & (core == self.core)


def enter(me, others=0):
    barrier = pltpu.get_barrier_semaphore()

    def greet(i):
        z, y, core = i // 8, (i // 2) % 4, i % 2

        @pl.when(jnp.logical_not(me.is_me(z, y, core)))
        def _():
            pl.semaphore_signal(barrier, 1, device_id=me.at(z, y, core), device_id_type=MESH)

    loop(64, greet)
    if others:

        def greet_other(i):
            here = i == 4
            z = jnp.where(here, me.z, i % 4 + 4 * (me.z // 4))
            core = jnp.where(here, 1 - me.core, me.core)
            pl.semaphore_signal(
                barrier, 1, device_id=me.at(z, me.y, core, 1 - me.plane), device_id_type=MESH
            )

        loop(others, greet_other)
    pl.semaphore_wait(barrier, 63 + others)


def send(src, dst, send_sem, recv_sem, device):
    return pltpu.make_async_remote_copy(
        src_ref=src, dst_ref=dst, send_sem=send_sem, recv_sem=recv_sem, device_id=device, device_id_type=MESH
    )


def arrived(ref, sem):
    pltpu.make_async_copy(ref, ref, sem).wait()


def start_either(here, remote, local):
    @pl.when(here)
    def _():
        local.start()

    @pl.when(jnp.logical_not(here))
    def _():
        remote.start()


def end_either(here, remote, local):
    @pl.when(jnp.logical_not(here))
    def _():
        remote.wait_send()


def spread_kernel(
    q_ref, k_ref, v_ref, lat_ref, gain_ref,
    qp_ref, kv_ref, lat_out, gain_out,
    q_in, qs, s_a, r_a, s_b, r_b, s_c, r_c, s_s, r_s, s_q, r_q, s_l, r_l, l_q,
):
    me = Place()
    z, y, core = me.z, me.y, me.core
    load_q = pltpu.make_async_copy(q_ref, q_in, l_q)
    load_q.start()
    enter(me)
    up, down = (y + 1) % 4, (y + 3) % 4
    mine = me.kv // 2 == core

    def order(j):
        odd = j % 2
        return odd * ((j + 1) // 2) + (1 - odd) * (8 - j // 2)

    def column(j, run):
        to_z = (z + order(j)) % 8

        @pl.when((to_z % 4) // 2 == core)
        def _():
            half = to_z % 2
            for part in range(PARTS):
                for kind in range(2):
                    first = part * PART
                    columns = pl.ds(pl.multiple_of(half * HEAD_DIM, HEAD_DIM), HEAD_DIM)
                    src = (k_ref, v_ref)[kind].at[pl.ds(first, PART), columns]
                    dst = kv_ref.at[kind, pl.ds(pl.multiple_of(me.ctx * 256 + first, PART), PART), :]
                    sem = r_a.at[part, z]
                    here = (to_z == z) & (core == kind)
                    copy = send(src, dst, s_a.at[part, kind, to_z], sem, me.at(to_z, y, kind))
                    run(here, copy, pltpu.make_async_copy(src, dst, sem))

    loop(AHEAD, lambda j: column(j, start_either))

    load_q.wait()

    def regroup(i):
        half, pair = i // 8, i % 8
        rows_at = pl.ds(pl.multiple_of(pair * 16, 16), 16)
        for block in range(2):
            tile = q_in[block, rows_at, pl.ds(pl.multiple_of(half * 512, 512), 512)].astype(F32)
            for part in range(2):
                rows = tile[part * 8 : part * 8 + 8]
                rows = jnp.concatenate([rows[:, h * 128 : h * 128 + 128] for h in range(4)], axis=0)
                qs[2 * i + part, block * ROWS : block * ROWS + ROWS, :] = rows.astype(BF16)

    loop(16, regroup)

    def query(j, run):
        i = (j + me.ctx) % 32
        to = me.worker(2 * core + i // 16, i % 16)
        run(
            me.is_me(*to),
            send(qs.at[i], qp_ref.at[me.ctx], s_q.at[i], r_q.at[me.ctx], me.at(*to)),
            pltpu.make_async_copy(qs.at[i], qp_ref.at[me.ctx], r_q.at[me.ctx]),
        )

    def rows_of(from_z, from_y, first=0, count=256):
        start = pl.multiple_of((from_z * 4 + from_y) * 256 + first, HALF)
        return kv_ref.at[core, pl.ds(start, count), :]

    def to_core(from_z):
        rows = kv_ref.at[core, pl.ds(pl.multiple_of(from_z * 1024, 1024), 1024), :]
        return send(rows, rows, s_s.at[from_z], r_s.at[from_z], me.at(z, y, 1 - core))

    def near(from_z, part):
        rows = rows_of(from_z, y, part * PART, PART)
        return (
            send(rows, rows, s_b.at[0, part, from_z], r_b.at[0, part, from_z], me.at(z, up, core)),
            send(rows, rows, s_b.at[1, part, from_z], r_b.at[1, part, from_z], me.at(z, down, core)),
        )

    def onward(from_z, part):
        one = rows_of(from_z, down, part * PART, HALF)
        two = rows_of(from_z, up, part * PART + HALF, HALF)
        return (
            send(one, one, s_c.at[0, part, from_z], r_c.at[0, part, from_z], me.at(z, up, core)),
            send(two, two, s_c.at[1, part, from_z], r_c.at[1, part, from_z], me.at(z, down, core)),
        )

    steps = 8 * PARTS

    def at_step(e):
        return (z + order(e // PARTS)) % 8, e % PARTS

    def ring(e):
        @pl.when(e < steps)
        def _():
            @pl.when((e % PARTS == 0) & (e // PARTS + AHEAD < 8))
            def _():
                column(e // PARTS + AHEAD, start_either)

            from_z, part = at_step(e)
            arrived(rows_of(from_z, y, part * PART, PART), r_a.at[part, from_z])
            for copy in near(from_z, part):
                copy.start()

        @pl.when((e >= Q_START) & (e < Q_START + 32 // Q_STEP))
        def _():
            for i in range(Q_STEP):
                query((e - Q_START) * Q_STEP + i, start_either)

        @pl.when((e >= LAG) & (e < steps + LAG))
        def _():
            from_z, part = at_step(e - LAG)
            copies = onward(from_z, part)
            arrived(rows_of(from_z, down, part * PART, PART), r_b.at[0, part, from_z])
            copies[0].start()
            arrived(rows_of(from_z, up, part * PART, PART), r_b.at[1, part, from_z])
            copies[1].start()

        @pl.when(e >= 2 * LAG)
        def _():
            from_z, part = at_step(e - 2 * LAG)
            opposite = (y + 2) % 4
            arrived(rows_of(from_z, opposite, part * PART, HALF), r_c.at[0, part, from_z])
            arrived(rows_of(from_z, opposite, part * PART + HALF, HALF), r_c.at[1, part, from_z])

            @pl.when(part == PARTS - 1)
            def _():
                to_core(from_z).start()

    loop(steps + 2 * LAG, ring)

    def pool_inputs():
        other = me.at(z, y, 1 - core)
        half = me.kv % 2
        lat = lat_ref.at[:, pl.ds(pl.multiple_of(half * 512, 512), 512)]
        gain = gain_ref.at[half]
        return (
            pltpu.make_async_copy(lat, lat_out, r_l.at[0]),
            pltpu.make_async_copy(gain, gain_out, r_l.at[1]),
            send(lat, lat_out, s_l.at[0], r_l.at[0], other),
            send(gain, gain_out, s_l.at[1], r_l.at[1], other),
        )

    @pl.when(mine)
    def _():
        for copy in pool_inputs():
            copy.start()

    loop(8, lambda j: column(j, end_either))

    def finish_ring(e):
        from_z, part = at_step(e)
        for copy in near(from_z, part) + onward(from_z, part):
            copy.wait_send()

    loop(steps, finish_ring)
    loop(32, lambda j: query(j, end_either))
    loop(32, lambda s: arrived(qp_ref.at[s], r_q.at[s]))

    def finish_core(from_z):
        to_core(from_z).wait_send()
        arrived(kv_ref.at[1 - core, pl.ds(pl.multiple_of(from_z * 1024, 1024), 1024), :], r_s.at[from_z])

    loop(8, finish_core)
    for copy in pool_inputs()[:2]:
        copy.wait()

    @pl.when(mine)
    def _():
        for copy in pool_inputs()[2:]:
            copy.wait_send()


def spread(queries, keys, values, latents, gain):
    dma = pltpu.SemaphoreType.DMA
    hbm = pl.BlockSpec(memory_space=pltpu.HBM)
    vmem = pl.BlockSpec(memory_space=pltpu.VMEM)
    return pl.pallas_call(
        spread_kernel,
        out_shape=(
            jax.ShapeDtypeStruct((32, 2 * ROWS, HEAD_DIM), BF16),
            jax.ShapeDtypeStruct((2, BLOCKS * BLOCK, HEAD_DIM), BF16),
            jax.ShapeDtypeStruct((512, 512), BF16),
            jax.ShapeDtypeStruct((4, 128), F32),
        ),
        in_specs=[hbm] * 5,
        out_specs=(vmem,) * 4,
        scratch_shapes=[
            pltpu.VMEM((2, BLOCK, 1024), BF16),
            pltpu.VMEM((32, 2 * ROWS, HEAD_DIM), BF16),
            dma((PARTS, 2, 8)), dma((PARTS, 8)),
            dma((2, PARTS, 8)), dma((2, PARTS, 8)),
            dma((2, PARTS, 8)), dma((2, PARTS, 8)),
            dma((8,)), dma((8,)),
            dma((32,)), dma((32,)),
            dma((2,)), dma((2,)),
            dma,
        ],
        compiler_params=pltpu.CompilerParams(
            collective_id=0, has_side_effects=True, vmem_limit_bytes=32 * 1024 * 1024
        ),
        name="spread",
    )(queries.reshape(2, BLOCK, 1024), keys, values, latents, gain)


def attend_kernel(doc_ref, source_ref, q_ref, kv_ref, out_ref, sq_ref, hot_ref, ka, va, qa, sq, hot, o_ref):
    first = lax.fori_loop(
        0,
        BLOCKS - LONG + 1,
        lambda i, found: jnp.where(doc_ref[i] == doc_ref[i + LONG - 1], i, found),
        jnp.int32(0),
    )

    def packed(i):
        return jnp.where(i < LONG, first + i, jnp.where(i - LONG < first, i - LONG, i))

    scale = math.log2(math.e) * HEAD_DIM ** (-0.5)

    def arrange(i):
        at = packed(i)
        here = pl.ds(pl.multiple_of(i * BLOCK, BLOCK), BLOCK)
        there = pl.ds(pl.multiple_of(at * BLOCK, BLOCK), BLOCK)
        key = kv_ref[0, there, :]
        ka[here, 0:128] = key
        ka[here, 128:256] = key
        va[here, 0:128] = kv_ref[1, there, :]
        va[here, 128:256] = jnp.ones((BLOCK, 128), BF16)
        query = q_ref[pl.ds(pl.multiple_of(at * ROWS, ROWS), ROWS), :].astype(F32) * scale
        high = query.astype(BF16)
        rows = pl.ds(pl.multiple_of(i * ROWS, ROWS), ROWS)
        qa[rows, 0:128] = high
        qa[rows, 128:256] = (query - high.astype(F32)).astype(BF16)

    loop(BLOCKS, arrange)

    def attend_rows(rows, base, chunks, docs=None):
        q = qa[rows, :]
        m = total = None
        for c in range(chunks):
            keys = slice(base + c * CHUNK, base + (c + 1) * CHUNK)
            s = lax.dot_general(q, ka[keys, :], (((1,), (1,)), ((), ())), preferred_element_type=F32)
            parts = [s[:, b * 128 : b * 128 + 128] for b in range(CHUNK // 128)]
            if docs is not None:
                for b in range(CHUNK // BLOCK):
                    key_doc = doc_ref[packed(jnp.int32((base + c * CHUNK) // BLOCK + b))]
                    parts[b] = jnp.where(docs == key_doc, parts[b], -1e30)
            top = functools.reduce(jnp.maximum, parts)
            top = jnp.broadcast_to(jnp.max(top, axis=1, keepdims=True), top.shape)
            new_m = top if m is None else jnp.maximum(m, top)
            w = jnp.concatenate([jnp.exp2(part - new_m).astype(BF16) for part in parts], axis=1)
            add = jnp.dot(w, va[keys, :], preferred_element_type=F32)
            if m is None:
                total = add
            else:
                shrink = jnp.exp2(m - new_m)
                total = total * jnp.concatenate([shrink, shrink], axis=1) + add
            m = new_m
        o_ref[rows, :] = (total[:, 0:128] / total[:, 128:256]).astype(BF16)

    def long_tile(t):
        attend_rows(pl.ds(pl.multiple_of(t * TILE, TILE), TILE), 0, LONG_KEYS // CHUNK)

    loop(LONG * ROWS // TILE, long_tile)

    def short_tile(t):
        per = SHORT_TILE // ROWS
        docs = jnp.concatenate(
            [jnp.full((ROWS, 128), doc_ref[packed(LONG + t * per + b)], jnp.int32) for b in range(per)], axis=0
        )
        rows = pl.ds(pl.multiple_of(LONG * ROWS + t * SHORT_TILE, 128), SHORT_TILE)
        attend_rows(rows, LONG_KEYS, SHORT_KEYS // CHUNK, docs)

    loop((BLOCKS - LONG) * ROWS // SHORT_TILE, short_tile)

    lanes = lax.broadcasted_iota(jnp.int32, (PIECE, 128), 1)

    def squares(half):
        part = sq[...]
        high = part.astype(BF16)
        low = (part - high.astype(F32)).astype(BF16)
        ones = jnp.ones((8, 128), BF16)
        dims = (((1,), (1,)), ((), ()))
        sq_ref[:, half * 256 : half * 256 + 256] = lax.dot_general(
            ones, high, dims, preferred_element_type=F32
        ) + lax.dot_general(ones, low, dims, preferred_element_type=F32)
        hot_ref[:, half * 256 : half * 256 + 256] = jnp.transpose(hot[...])[0:DOCS].astype(BF16)

    for half in range(2):
        def move_half(i, half=half):
            p = half * 32 + i
            at = source_ref[p]
            doc = doc_ref[at]
            row = jnp.where(at < first, at + LONG, jnp.where(at < first + LONG, at - first, at))
            piece = o_ref[pl.ds(pl.multiple_of(row * ROWS, ROWS), ROWS), :]
            out_ref[p] = piece
            wide = piece.astype(F32)
            wide = wide * wide
            here = pl.ds(pl.multiple_of(i * PIECE, PIECE), PIECE)
            sq[here, :] = wide[0:8] + wide[8:16] + wide[16:24] + wide[24:32]
            hot[here, :] = (lanes == doc).astype(F32)

        loop(32, move_half)
        squares(half)


def attend(block_doc, block_source, q, kv):
    smem = pl.BlockSpec(memory_space=pltpu.SMEM)
    vmem = pl.BlockSpec(memory_space=pltpu.VMEM)
    return pl.pallas_call(
        attend_kernel,
        out_shape=(
            jax.ShapeDtypeStruct((BLOCKS, ROWS, HEAD_DIM), BF16),
            jax.ShapeDtypeStruct((8, BLOCKS * PIECE), F32),
            jax.ShapeDtypeStruct((DOCS, BLOCKS * PIECE), BF16),
        ),
        in_specs=[smem, smem, vmem, vmem],
        out_specs=(vmem, vmem, vmem),
        scratch_shapes=[
            pltpu.VMEM((BLOCKS * BLOCK, 256), BF16),
            pltpu.VMEM((BLOCKS * BLOCK, 256), BF16),
            pltpu.VMEM((BLOCKS * ROWS, 256), BF16),
            pltpu.VMEM((256, 128), F32),
            pltpu.VMEM((256, 128), F32),
            pltpu.VMEM((BLOCKS * ROWS, HEAD_DIM), BF16),
        ],
        compiler_params=pltpu.CompilerParams(vmem_limit_bytes=48 * 1024 * 1024),
        name="attend",
    )(block_doc, block_source, q, kv)


def collect_kernel(
    o_ref, sq_ref, hot_ref, lat_ref, gain_ref,
    att_ref, emb_ref,
    home, sq_in, doc_out, doc_in, norm_out, norm_in, row_out, row_in,
    s_o, r_o, s_sq, r_sq, s_d, r_d, s_n, r_n, s_e, r_e,
):
    me = Place()
    enter(me, 5)
    me8 = me.plane * 4 + me.kv
    core = me.core
    to_core = me.kv // 2
    half = me.kv % 2

    def partners(src, box, s_sem, r_sem, run):
        def one(i):
            @pl.when(i != me8)
            def _():
                device = me.at(i % 4 + 4 * (me.z // 4), me.y, me.core, i // 4)
                run(send(src, box.at[me8], s_sem.at[i], r_sem.at[me8], device))

        loop(8, one)

    def from_partners(box, r_sem):
        def one(i):
            @pl.when(i != me8)
            def _():
                arrived(box.at[i], r_sem.at[i])

        loop(8, one)

    start = lambda copy: copy.start()
    sent = lambda copy: copy.wait_send()

    partners(sq_ref, sq_in, s_sq, r_sq, start)
    sq_in[me8] = sq_ref[...]

    def result(j, run):
        s = (j + me.ctx) % 32
        src = o_ref.at[pl.ds(2 * s, 2)]
        slot = half * 16 + me.piece
        run(
            me.is_me(s // 4, s % 4, to_core),
            send(src, home.at[slot], s_o.at[s], r_o.at[slot], me.at(s // 4, s % 4, to_core)),
            pltpu.make_async_copy(src, home.at[slot], r_o.at[slot]),
        )

    loop(32, lambda j: result(j, start_either))

    from_partners(sq_in, r_sq)
    channel_total = jnp.sum(sq_in[...], axis=0)[0:1]
    factor = lax.rsqrt(channel_total / CHANNELS + EPS)
    factor = jnp.transpose(jnp.broadcast_to(factor, (128, BLOCKS * PIECE)))
    whole = o_ref[...].astype(F32).reshape(BLOCKS, 4, PIECE, 128)
    normed = []
    for h in range(4):
        part = whole[:, h].reshape(BLOCKS * PIECE, 128)
        normed.append((part * factor * gain_ref[h : h + 1, :]).astype(BF16))
    normed = jnp.concatenate(normed, axis=1)

    lat = lat_ref[...]
    s = lax.dot_general(normed, lat, (((1,), (1,)), ((), ())), preferred_element_type=F32) * 512 ** (-0.5)
    w = jnp.exp(s - jnp.max(s, axis=-1, keepdims=True))
    w = (w / jnp.sum(w, axis=-1, keepdims=True)).astype(BF16)
    by_doc = jnp.dot(hot_ref[...], w, preferred_element_type=F32)
    sums = None
    for _ in range(3):
        part = by_doc.astype(BF16)
        by_doc = by_doc - part.astype(F32)
        add = jnp.dot(part, lat, preferred_element_type=F32)
        sums = add if sums is None else sums + add

    w8 = me.piece % 8
    doc_out[...] = jnp.concatenate(
        [
            sums[two * 8 : two * 8 + 8, h * 128 : h * 128 + 128].reshape(8, 1, 128)
            for two in range(2)
            for h in range(4)
        ],
        axis=1,
    )

    def document(w, run):
        run(
            w == w8,
            send(doc_out.at[w], doc_in.at[w8], s_d.at[w], r_d.at[w8], me.at(me.z, w // 2, w % 2)),
            pltpu.make_async_copy(doc_out.at[w], doc_in.at[w8], r_d.at[w8]),
        )

    loop(8, lambda w: document(w, start_either))
    loop(8, lambda w: arrived(doc_in.at[w], r_d.at[w]))
    row_out[...] = jnp.sum(doc_in[...], axis=0)

    def share(j, run):
        s = (j + me.ctx) % 32
        dst = row_in.at[half, me.piece]
        slot = half * 16 + me.piece
        run(
            me.is_me(s // 4, s % 4, to_core),
            send(row_out, dst, s_e.at[s], r_e.at[slot], me.at(s // 4, s % 4, to_core)),
            pltpu.make_async_copy(row_out, dst, r_e.at[slot]),
        )

    loop(32, lambda j: share(j, start_either))

    loop(32, lambda i: arrived(home.at[i], r_o.at[i]))
    for side in range(2):
        for block in range(2):
            for pair in range(8):
                rows = []
                for part in range(2):
                    piece = home[side * 16 + pair * 2 + part, block].astype(F32)
                    rows.append(jnp.concatenate([piece[h * 8 : h * 8 + 8] for h in range(4)], axis=1))
                at = block * BLOCK + pair * 16
                att_ref[at : at + 16, side * 512 : side * 512 + 512] = jnp.concatenate(rows, axis=0).astype(BF16)

    loop(32, lambda i: arrived(row_in.at[i // 16, i % 16], r_e.at[i]))
    rows = row_in[...]
    rows = rows[:, 0:8] + rows[:, 8:16]
    for two in range(2):
        square = rows[:, :, two * 4 : two * 4 + 4, :]
        square = jnp.sum(square * square, axis=(0, 2))
        norm_out[two] = jnp.broadcast_to(jnp.sum(square, axis=-1, keepdims=True), (8, 128))
    my_head = me.plane * 2 + core

    def head(i, run):
        @pl.when(i != my_head)
        def _():
            device = me.at(me.z, me.y, i % 2, i // 2)
            run(send(norm_out, norm_in.at[my_head], s_n.at[i], r_n.at[my_head], device))

    loop(4, lambda i: head(i, start))
    norm_in[my_head] = norm_out[...]

    def from_head(i):
        @pl.when(i != my_head)
        def _():
            arrived(norm_in.at[i], r_n.at[i])

    loop(4, from_head)
    factors = lax.rsqrt(jnp.sum(norm_in[...], axis=0) / CHANNELS + EPS)
    for side in range(2):
        for h in range(4):
            at = side * 512 + h * 128
            for two in range(2):
                emb_ref[two * 8 : two * 8 + 8, at : at + 128] = rows[side, :, two * 4 + h, :] * factors[two]

    partners(sq_ref, sq_in, s_sq, r_sq, sent)
    loop(4, lambda i: head(i, sent))
    loop(32, lambda j: result(j, end_either))
    loop(8, lambda w: document(w, end_either))
    loop(32, lambda j: share(j, end_either))


def collect(results, squares, hot, latents, gain):
    dma = pltpu.SemaphoreType.DMA
    vmem = pl.BlockSpec(memory_space=pltpu.VMEM)
    return pl.pallas_call(
        collect_kernel,
        out_shape=(
            jax.ShapeDtypeStruct((256, 1024), BF16),
            jax.ShapeDtypeStruct((DOCS, 1024), F32),
        ),
        in_specs=[vmem] * 5,
        out_specs=(vmem, vmem),
        scratch_shapes=[
            pltpu.VMEM((32, 2, ROWS, HEAD_DIM), BF16),
            pltpu.VMEM((8, 8, BLOCKS * PIECE), F32),
            pltpu.VMEM((8, 8, 128), F32),
            pltpu.VMEM((8, 8, 128), F32),
            pltpu.VMEM((2, 8, 128), F32),
            pltpu.VMEM((4, 2, 8, 128), F32),
            pltpu.VMEM((8, 128), F32),
            pltpu.VMEM((2, 16, 8, 128), F32),
            dma((32,)), dma((32,)),
            dma((8,)), dma((8,)),
            dma((8,)), dma((8,)),
            dma((4,)), dma((4,)),
            dma((32,)), dma((32,)),
        ],
        compiler_params=pltpu.CompilerParams(
            collective_id=1, has_side_effects=True, vmem_limit_bytes=40 * 1024 * 1024
        ),
        name="collect",
    )(results, squares, hot, latents, gain)


def shards(queries, keys, values, latents, norm_gain, block_doc, block_source):
    q, kv, lat, gain = spread(queries, keys, values, latents, norm_gain.reshape(2, 4, 128))
    results, squares, hot = attend(block_doc, block_source, q.reshape(BLOCKS * ROWS, HEAD_DIM), kv)
    return collect(results, squares, hot, lat, gain)


def solution(mesh):
    in_specs = (
        P(("dp", "ctx"), "head"),
        P(("dp", "ctx"), "head"),
        P(("dp", "ctx"), "head"),
        P(None, "head"),
        P("head"),
        P("dp"),
        P("dp"),
    )
    out_specs = (P(("dp", "ctx"), "head"), P("dp", "head"))
    return jax.shard_map(shards, mesh=mesh, in_specs=in_specs, out_specs=out_specs, check_vma=False)
```

time: 124 us -> 108 us (0.87)
  Pallas kernels: 116 us -> 99.5 us
    pallas_call x1, Pallas kernels: 24.8 us -> 15.7 us  [attend(): pl.pallas_call(attend_kernel, out_shape=(jax.ShapeDtypeStruct((BLOCKS, RO...]
    pallas_call x1, Pallas kernels: 43.6 us -> 38.1 us  [collect(): pl.pallas_call(collect_kernel, out_shape=(jax.ShapeDtypeStruct((256, 1024...]
    pallas_call x1, Pallas kernels: 47.4 us -> 45.7 us  [spread(): pl.pallas_call(spread_kernel, out_shape=(jax.ShapeDtypeStruct((32, 2 * RO...]
where the time goes in v2:
time: 108 us
  Pallas kernels  99.5 us (92%)
  local copies, waits for them, and re-layouts  7.48 us (7%)
    pallas_call x1, Pallas kernels, spread(): pl.pallas_call(spread_kernel, out_shape=(jax.ShapeDtypeStruct((32, 2 * RO...  45.7 us
    pallas_call x1, Pallas kernels, collect(): pl.pallas_call(collect_kernel, out_shape=(jax.ShapeDtypeStruct((256, 1024...  38.1 us
    pallas_call x1, Pallas kernels, attend(): pl.pallas_call(attend_kernel, out_shape=(jax.ShapeDtypeStruct((BLOCKS, RO...  15.7 us
    unnamed x16, local copies, waits for them, and re-layouts  7.48 us

profile of v2, /device:TPU:1, one launch (start us, length us, event | category | flops | bytes accessed | tf_op | source)
XLA Modules:
  0.0 107.6 jit_solution(5121439618961923201)
XLA Ops:
  0.6 0.0 copy-start
  0.6 1.2 %copy-done = bf16[512,1024]{1,0:T(8,128)(2,1)S(1)} copy-done((bf16[512,1024]{1,0:T(8,128)(2,1)S(1)}, bf16[512,1024]{1,0:T(8,128)(2,1)}, u32[]{:S(2)}) %copy-start) | copy-done | bytes 1048600
  1.9 0.0 copy-start.1
  1.9 1.0 copy-done.1
  2.9 0.0 copy-start.2
  2.9 0.9 copy-done.2
  3.8 0.0 copy-start.3
  3.8 0.9 copy-done.3
  4.7 0.0 copy-start.4
  4.7 0.7 copy-done.4
  5.4 45.7 %spread.1 = (bf16[32,64,128]{2,1,0:T(8,128)(2,1)S(1)}, bf16[2,8192,128]{2,1,0:T(8,128)(2,1)S(1)}, bf16[512,512]{1,0:T(8,128)(2,1)S(1)}, f32[4,128]{1,0:T(4,128)S(1)}) custom-call(bf16[2,128,1024]{2,1,0:T(8,128)(2,1)S(1)} %bitcast.3, bf16[256,256]{1,0:T(8,128)(2,1)S(1)} %copy-done.2, bf16[256,256]{1,0:T(8,128)(2,1)S(1)} %copy-done.3, ...), custom_call_target="tpu_custom_call" | custom-call | tf_op jit(solution)/shard_map/spread/pallas_call | solution.py:291
  51.1 0.0 copy-start.5
  51.1 0.6 copy-done.5
  51.7 0.0 copy-start.6
  51.7 0.7 copy-done.6
  52.4 15.7 %attend.1 = (bf16[64,32,128]{2,1,0:T(8,128)(2,1)S(1)}, f32[8,512]{1,0:T(8,128)S(1)}, bf16[16,512]{1,0:T(8,128)(2,1)S(1)}) custom-call(s32[64]{0:T(128)S(1)} %copy-done.5, s32[64]{0:T(128)S(1)} %copy-done.6, bf16[2048,128]{1,0:T(8,128)(2,1)S(1)} %bitcast.4, bf16[2,8192,128]{2,1,0:T(8,128)(2,1)S(1)} %get-tuple-element.10.kv_ref), custom_call_target="tpu_custom_call" | custom-call | tf_op jit(solution)/shard_map/attend/pallas_call | solution.py:422
  68.0 38.1 %collect.1 = (bf16[256,1024]{1,0:T(8,128)(2,1)S(1)}, f32[16,1024]{1,0:T(8,128)S(1)}) custom-call(bf16[64,32,128]{2,1,0:T(8,128)(2,1)S(1)} %get-tuple-element.11.o_ref, f32[8,512]{1,0:T(8,128)S(1)} %get-tuple-element.12.sq_ref, bf16[16,512]{1,0:T(8,128)(2,1)S(1)} %get-tuple-element.13.hot_ref, bf16[512,512]{1,0:T(8,128)(2,1)S(1)} %get-tuple-element.14.lat_ref, ...), custom_call_target="tpu_custom_call" | custom-call | tf_op jit(solution)/shard_map/collect/pallas_call | solution.py:600
  106.2 0.8 copy.11
  107.0 0.6 copy.12
Async XLA Ops:
  0.6 1.2 %copy-start = (bf16[512,1024]{1,0:T(8,128)(2,1)S(1)}, bf16[512,1024]{1,0:T(8,128)(2,1)}, u32[]{:S(2)}) copy-start(bf16[512,1024]{1,0:T(8,128)(2,1)} %lat_ref.1) | copy-start | bytes 3145732
  1.9 1.0 copy-start.1
  2.9 0.9 copy-start.2
  3.8 0.9 copy-start.3
  4.7 0.7 copy-start.4
  51.1 0.7 copy-start.5
  51.7 0.7 copy-start.6

commit v3 on v2

v3 whole, which is shorter than its diff:
```python
import functools
import math

import jax
import jax.numpy as jnp
from jax import lax
from jax.experimental import pallas as pl
from jax.experimental.pallas import tpu as pltpu
from jax.sharding import PartitionSpec as P

HEADS = 32
HEAD_DIM = 128
BLOCK = 128
BLOCKS = 64
LONG = 40
DOCS = 16
CHANNELS = HEADS * HEAD_DIM
PIECE = 8
ROWS = 4 * PIECE
TILE = 640
SHORT_TILE = 384
CHUNK = 256
LONG_KEYS = LONG * BLOCK
SHORT_KEYS = (BLOCKS - LONG) * BLOCK
EPS = 1e-05
PARTS = 1
PART = 256 // PARTS
HALF = PART // 2
AHEAD = 4
Q_START = 4
Q_STEP = 4
LAG = 4
MESH = pl.DeviceIdType.MESH
F32 = jnp.float32
BF16 = jnp.bfloat16


def loop(count, body):
    def step(i, carry):
        body(i)
        return carry

    lax.fori_loop(0, count, step, 0)


class Place:
    def __init__(self):
        self.ctx = lax.axis_index("ctx")
        head = lax.axis_index("head")
        self.z = self.ctx // 4
        self.y = self.ctx % 4
        self.plane = head // 2
        self.core = head % 2
        self.kv = self.z % 4
        self.piece = (self.z // 4) * 8 + self.y * 2 + self.core

    def at(self, z, y, core, plane=None):
        plane = self.plane if plane is None else plane
        return {"ctx": z * 4 + y, "head": plane * 2 + core}

    def worker(self, kv, piece):
        return (kv + 4 * (piece // 8), (piece % 8) // 2, piece % 2)

    def is_me(self, z, y, core):
        return (z == self.z) & (y == self.y) & (core == self.core)


def greet(me):
    barrier = pltpu.get_barrier_semaphore()

    def one(i):
        z, y, core = i // 8, (i // 2) % 4, i % 2

        @pl.when(jnp.logical_not(me.is_me(z, y, core)))
        def _():
            pl.semaphore_signal(barrier, 1, device_id=me.at(z, y, core), device_id_type=MESH)

    def other(i):
        here = i == 4
        z = jnp.where(here, me.z, i % 4 + 4 * (me.z // 4))
        core = jnp.where(here, 1 - me.core, me.core)
        pl.semaphore_signal(barrier, 1, device_id=me.at(z, me.y, core, 1 - me.plane), device_id_type=MESH)

    loop(64, one)
    loop(5, other)
    return barrier


def send(src, dst, send_sem, recv_sem, device):
    return pltpu.make_async_remote_copy(
        src_ref=src, dst_ref=dst, send_sem=send_sem, recv_sem=recv_sem, device_id=device, device_id_type=MESH
    )


def arrived(ref, sem):
    pltpu.make_async_copy(ref, ref, sem).wait()


def start_either(here, remote, local):
    @pl.when(here)
    def _():
        local.start()

    @pl.when(jnp.logical_not(here))
    def _():
        remote.start()


def end_either(here, remote, local):
    @pl.when(jnp.logical_not(here))
    def _():
        remote.wait_send()


def kernel(
    doc_ref, source_ref, q_ref, k_ref, v_ref, lat_ref, gain_ref,
    att_ref, emb_ref,
    q_in, qs, qp, kv, lat_in, gain_in, ka, va, qa, o_ref, res,
    home, sq_out, sq_in, doc_out, doc_in, norm_out, norm_in, row_out, row_in,
    s_a, r_a, s_b, r_b, s_c, r_c, s_s, r_s, s_q, r_q, s_l, r_l, l_q,
    s_o, r_o, s_sq, r_sq, s_d, r_d, s_n, r_n, s_e, r_e,
):
    me = Place()
    z, y, core = me.z, me.y, me.core
    load_q = pltpu.make_async_copy(q_ref, q_in, l_q)
    load_q.start()
    barrier = greet(me)

    load_q.wait()

    def regroup(i):
        half, pair = i // 8, i % 8
        rows_at = pl.ds(pl.multiple_of(pair * 16, 16), 16)
        for block in range(2):
            tile = q_in[block, rows_at, pl.ds(pl.multiple_of(half * 512, 512), 512)].astype(F32)
            for part in range(2):
                rows = tile[part * 8 : part * 8 + 8]
                rows = jnp.concatenate([rows[:, h * 128 : h * 128 + 128] for h in range(4)], axis=0)
                qs[2 * i + part, block * ROWS : block * ROWS + ROWS, :] = rows.astype(BF16)

    loop(16, regroup)
    va[:, :, 128:256] = jnp.ones((BLOCKS, BLOCK, 128), BF16)

    first = jnp.int32(0)
    for i in range(BLOCKS - LONG + 1):
        first = jnp.where(doc_ref[i] == doc_ref[i + LONG - 1], i, first)

    def packed(i):
        return jnp.where(i < LONG, first + i, jnp.where(i - LONG < first, i - LONG, i))

    def sorted_place(at):
        return jnp.where(at < first, at + LONG, jnp.where(at < first + LONG, at - first, at))

    pl.semaphore_wait(barrier, 68)

    up, down = (y + 1) % 4, (y + 3) % 4
    mine = me.kv // 2 == core

    def order(j):
        odd = j % 2
        return odd * ((j + 1) // 2) + (1 - odd) * (8 - j // 2)

    def column(j, run):
        to_z = (z + order(j)) % 8

        @pl.when((to_z % 4) // 2 == core)
        def _():
            half = to_z % 2
            for part in range(PARTS):
                for kind in range(2):
                    first = part * PART
                    columns = pl.ds(pl.multiple_of(half * HEAD_DIM, HEAD_DIM), HEAD_DIM)
                    src = (k_ref, v_ref)[kind].at[pl.ds(first, PART), columns]
                    dst = kv.at[kind, pl.ds(pl.multiple_of(me.ctx * 256 + first, PART), PART), :]
                    sem = r_a.at[part, z]
                    here = (to_z == z) & (core == kind)
                    copy = send(src, dst, s_a.at[part, kind, to_z], sem, me.at(to_z, y, kind))
                    run(here, copy, pltpu.make_async_copy(src, dst, sem))

    loop(AHEAD, lambda j: column(j, start_either))

    def query(j, run):
        i = (j + me.ctx) % 32
        to = me.worker(2 * core + i // 16, i % 16)
        run(
            me.is_me(*to),
            send(qs.at[i], qp.at[me.ctx], s_q.at[i], r_q.at[me.ctx], me.at(*to)),
            pltpu.make_async_copy(qs.at[i], qp.at[me.ctx], r_q.at[me.ctx]),
        )

    def rows_of(from_z, from_y, first=0, count=256):
        start = pl.multiple_of((from_z * 4 + from_y) * 256 + first, HALF)
        return kv.at[core, pl.ds(start, count), :]

    def to_core(from_z):
        rows = kv.at[core, pl.ds(pl.multiple_of(from_z * 1024, 1024), 1024), :]
        return send(rows, rows, s_s.at[from_z], r_s.at[from_z], me.at(z, y, 1 - core))

    def near(from_z, part):
        rows = rows_of(from_z, y, part * PART, PART)
        return (
            send(rows, rows, s_b.at[0, part, from_z], r_b.at[0, part, from_z], me.at(z, up, core)),
            send(rows, rows, s_b.at[1, part, from_z], r_b.at[1, part, from_z], me.at(z, down, core)),
        )

    def onward(from_z, part):
        one = rows_of(from_z, down, part * PART, HALF)
        two = rows_of(from_z, up, part * PART + HALF, HALF)
        return (
            send(one, one, s_c.at[0, part, from_z], r_c.at[0, part, from_z], me.at(z, up, core)),
            send(two, two, s_c.at[1, part, from_z], r_c.at[1, part, from_z], me.at(z, down, core)),
        )

    steps = 8 * PARTS

    def at_step(e):
        return (z + order(e // PARTS)) % 8, e % PARTS

    def ring(e):
        @pl.when(e < steps)
        def _():
            @pl.when((e % PARTS == 0) & (e // PARTS + AHEAD < 8))
            def _():
                column(e // PARTS + AHEAD, start_either)

            from_z, part = at_step(e)
            arrived(rows_of(from_z, y, part * PART, PART), r_a.at[part, from_z])
            for copy in near(from_z, part):
                copy.start()

        @pl.when((e >= Q_START) & (e < Q_START + 32 // Q_STEP))
        def _():
            for i in range(Q_STEP):
                query((e - Q_START) * Q_STEP + i, start_either)

        @pl.when((e >= LAG) & (e < steps + LAG))
        def _():
            from_z, part = at_step(e - LAG)
            copies = onward(from_z, part)
            arrived(rows_of(from_z, down, part * PART, PART), r_b.at[0, part, from_z])
            copies[0].start()
            arrived(rows_of(from_z, up, part * PART, PART), r_b.at[1, part, from_z])
            copies[1].start()

        @pl.when(e >= 2 * LAG)
        def _():
            from_z, part = at_step(e - 2 * LAG)
            opposite = (y + 2) % 4
            arrived(rows_of(from_z, opposite, part * PART, HALF), r_c.at[0, part, from_z])
            arrived(rows_of(from_z, opposite, part * PART + HALF, HALF), r_c.at[1, part, from_z])

            @pl.when(part == PARTS - 1)
            def _():
                to_core(from_z).start()

    loop(steps + 2 * LAG, ring)

    def pool_inputs():
        other = me.at(z, y, 1 - core)
        half = me.kv % 2
        lat = lat_ref.at[:, pl.ds(pl.multiple_of(half * 512, 512), 512)]
        gain = gain_ref.at[half]
        return (
            pltpu.make_async_copy(lat, lat_in, r_l.at[0]),
            pltpu.make_async_copy(gain, gain_in, r_l.at[1]),
            send(lat, lat_in, s_l.at[0], r_l.at[0], other),
            send(gain, gain_in, s_l.at[1], r_l.at[1], other),
        )

    @pl.when(mine)
    def _():
        for copy in pool_inputs():
            copy.start()

    def sends_done():
        loop(8, lambda j: column(j, end_either))

        def ring_done(e):
            from_z, part = at_step(e)
            for copy in near(from_z, part) + onward(from_z, part):
                copy.wait_send()

        loop(steps, ring_done)
        loop(32, lambda j: query(j, end_either))
        loop(8, lambda from_z: to_core(from_z).wait_send())

        @pl.when(mine)
        def _():
            for copy in pool_inputs()[2:]:
                copy.wait_send()

    def arrange_keys(j):
        from_z = (z + order(j)) % 8
        rows = pl.ds(pl.multiple_of(from_z * 1024, 1024), 1024)
        blocks = pl.ds(from_z * 8, 8)
        arrived(kv.at[1 - core, rows, :], r_s.at[from_z])
        key = kv[0, rows, :].reshape(8, BLOCK, 128)
        ka[blocks, :, 0:128] = key
        ka[blocks, :, 128:256] = key
        va[blocks, :, 0:128] = kv[1, rows, :].reshape(8, BLOCK, 128)

    scale = math.log2(math.e) * HEAD_DIM ** (-0.5)

    def arrange_queries(s):
        arrived(qp.at[s], r_q.at[s])
        query = qp[s].reshape(2, ROWS, 128).astype(F32) * scale
        high = query.astype(BF16)
        blocks = pl.ds(2 * s, 2)
        qa[blocks, :, 0:128] = high
        qa[blocks, :, 128:256] = (query - high.astype(F32)).astype(BF16)

    loop(32, arrange_queries)
    loop(8, arrange_keys)

    sends_done()
    for copy in pool_inputs()[:2]:
        copy.wait()

    def blocks_of(ref, first_block, count):
        return jnp.concatenate([ref[packed(first_block + b)] for b in range(count)], axis=0)

    def attend_rows(q, keys_at, chunks, rows, docs=None):
        m = total = None
        for c in range(chunks):
            key, value, key_docs = keys_at(c)
            s = lax.dot_general(q, key, (((1,), (1,)), ((), ())), preferred_element_type=F32)
            parts = [s[:, b * 128 : b * 128 + 128] for b in range(CHUNK // 128)]
            if docs is not None:
                parts = [jnp.where(docs == doc, part, -1e30) for doc, part in zip(key_docs, parts)]
            top = functools.reduce(jnp.maximum, parts)
            top = jnp.broadcast_to(jnp.max(top, axis=1, keepdims=True), top.shape)
            new_m = top if m is None else jnp.maximum(m, top)
            w = jnp.concatenate([jnp.exp2(part - new_m).astype(BF16) for part in parts], axis=1)
            add = jnp.dot(w, value, preferred_element_type=F32)
            if m is None:
                total = add
            else:
                shrink = jnp.exp2(m - new_m)
                total = total * jnp.concatenate([shrink, shrink], axis=1) + add
            m = new_m
        o_ref[rows] = (total[:, 0:128] / total[:, 128:256]).astype(BF16).reshape(-1, ROWS, 128)

    per_chunk = CHUNK // BLOCK

    def long_keys(c):
        return blocks_of(ka, c * per_chunk, per_chunk), blocks_of(va, c * per_chunk, per_chunk), None

    def long_tile(t):
        per = TILE // ROWS
        attend_rows(blocks_of(qa, t * per, per), long_keys, LONG_KEYS // CHUNK, pl.ds(t * per, per))

    def short_keys(c):
        at = LONG + c * per_chunk
        docs = [doc_ref[packed(at + b)] for b in range(per_chunk)]
        return blocks_of(ka, at, per_chunk), blocks_of(va, at, per_chunk), docs

    def short_tile(t):
        per = SHORT_TILE // ROWS
        at = LONG + t * per
        docs = jnp.concatenate([jnp.full((ROWS, 128), doc_ref[packed(at + b)], jnp.int32) for b in range(per)], axis=0)
        attend_rows(blocks_of(qa, at, per), short_keys, SHORT_KEYS // CHUNK, pl.ds(at, per), docs)

    loop((BLOCKS - LONG) * ROWS // SHORT_TILE, short_tile)
    loop(LONG * ROWS // TILE, long_tile)

    whole = o_ref[...].astype(F32).reshape(BLOCKS, 4, PIECE, 128)
    square = jnp.sum(whole * whole, axis=1).reshape(BLOCKS * PIECE, 128)
    high = square.astype(BF16)
    low = (square - high.astype(F32)).astype(BF16)
    ones = jnp.ones((8, 128), BF16)
    dims = (((1,), (1,)), ((), ()))
    sq_out[...] = lax.dot_general(ones, high, dims, preferred_element_type=F32) + lax.dot_general(
        ones, low, dims, preferred_element_type=F32
    )

    me8 = me.plane * 4 + me.kv
    home_core = me.kv // 2
    half = me.kv % 2

    def partners(src, box, s_sem, r_sem, run):
        def one(i):
            @pl.when(i != me8)
            def _():
                device = me.at(i % 4 + 4 * (me.z // 4), me.y, me.core, i // 4)
                run(send(src, box.at[me8], s_sem.at[i], r_sem.at[me8], device))

        loop(8, one)

    def from_partners(box, r_sem):
        def one(i):
            @pl.when(i != me8)
            def _():
                arrived(box.at[i], r_sem.at[i])

        loop(8, one)

    start = lambda copy: copy.start()
    sent = lambda copy: copy.wait_send()

    partners(sq_out, sq_in, s_sq, r_sq, start)
    sq_in[me8] = sq_out[...]

    def result(j, run):
        s = (j + me.ctx) % 32
        src = res.at[pl.ds(2 * s, 2)]
        slot = half * 16 + me.piece
        run(
            me.is_me(s // 4, s % 4, home_core),
            send(src, home.at[slot], s_o.at[s], r_o.at[slot], me.at(s // 4, s % 4, home_core)),
            pltpu.make_async_copy(src, home.at[slot], r_o.at[slot]),
        )

    def move(p):
        res[p] = o_ref[sorted_place(source_ref[p])]

    loop(BLOCKS, move)
    loop(32, lambda j: result(j, start_either))

    from_partners(sq_in, r_sq)
    channel_total = jnp.sum(sq_in[...], axis=0)[0:1]
    factor = lax.rsqrt(channel_total / CHANNELS + EPS)
    factor = jnp.transpose(jnp.broadcast_to(factor, (128, BLOCKS * PIECE)))
    whole = o_ref[...].astype(F32).reshape(BLOCKS, 4, PIECE, 128)
    normed = []
    for h in range(4):
        part = whole[:, h].reshape(BLOCKS * PIECE, 128)
        normed.append((part * factor * gain_in[h : h + 1, :]).astype(BF16))
    normed = jnp.concatenate(normed, axis=1)

    lat = lat_in[...]
    s = lax.dot_general(normed, lat, (((1,), (1,)), ((), ())), preferred_element_type=F32) * 512 ** (-0.5)
    w = jnp.exp(s - jnp.max(s, axis=-1, keepdims=True))
    w = (w / jnp.sum(w, axis=-1, keepdims=True)).astype(BF16)
    tokens = lax.broadcasted_iota(jnp.int32, (DOCS, PIECE), 0)
    hot = jnp.concatenate(
        [(tokens == doc_ref[packed(i)]).astype(F32) for i in range(BLOCKS)], axis=1
    ).astype(BF16)
    by_doc = jnp.dot(hot, w, preferred_element_type=F32)
    sums = None
    for _ in range(3):
        part = by_doc.astype(BF16)
        by_doc = by_doc - part.astype(F32)
        add = jnp.dot(part, lat, preferred_element_type=F32)
        sums = add if sums is None else sums + add

    w8 = me.piece % 8
    doc_out[...] = jnp.concatenate(
        [
            sums[two * 8 : two * 8 + 8, h * 128 : h * 128 + 128].reshape(8, 1, 128)
            for two in range(2)
            for h in range(4)
        ],
        axis=1,
    )

    def document(w, run):
        run(
            w == w8,
            send(doc_out.at[w], doc_in.at[w8], s_d.at[w], r_d.at[w8], me.at(me.z, w // 2, w % 2)),
            pltpu.make_async_copy(doc_out.at[w], doc_in.at[w8], r_d.at[w8]),
        )

    loop(8, lambda w: document(w, start_either))
    loop(8, lambda w: arrived(doc_in.at[w], r_d.at[w]))
    row_out[...] = jnp.sum(doc_in[...], axis=0)

    def share(j, run):
        s = (j + me.ctx) % 32
        dst = row_in.at[half, me.piece]
        slot = half * 16 + me.piece
        run(
            me.is_me(s // 4, s % 4, home_core),
            send(row_out, dst, s_e.at[s], r_e.at[slot], me.at(s // 4, s % 4, home_core)),
            pltpu.make_async_copy(row_out, dst, r_e.at[slot]),
        )

    loop(32, lambda j: share(j, start_either))

    loop(32, lambda i: arrived(home.at[i], r_o.at[i]))
    for side in range(2):
        for block in range(2):
            for pair in range(8):
                rows = []
                for part in range(2):
                    piece = home[side * 16 + pair * 2 + part, block].astype(F32)
                    rows.append(jnp.concatenate([piece[h * 8 : h * 8 + 8] for h in range(4)], axis=1))
                at = block * BLOCK + pair * 16
                att_ref[at : at + 16, side * 512 : side * 512 + 512] = jnp.concatenate(rows, axis=0).astype(BF16)

    loop(32, lambda i: arrived(row_in.at[i // 16, i % 16], r_e.at[i]))
    rows = row_in[...]
    rows = rows[:, 0:8] + rows[:, 8:16]
    for two in range(2):
        square = rows[:, :, two * 4 : two * 4 + 4, :]
        square = jnp.sum(square * square, axis=(0, 2))
        norm_out[two] = jnp.broadcast_to(jnp.sum(square, axis=-1, keepdims=True), (8, 128))
    my_head = me.plane * 2 + core

    def head(i, run):
        @pl.when(i != my_head)
        def _():
            device = me.at(me.z, me.y, i % 2, i // 2)
            run(send(norm_out, norm_in.at[my_head], s_n.at[i], r_n.at[my_head], device))

    loop(4, lambda i: head(i, start))
    norm_in[my_head] = norm_out[...]

    def from_head(i):
        @pl.when(i != my_head)
        def _():
            arrived(norm_in.at[i], r_n.at[i])

    loop(4, from_head)
    factors = lax.rsqrt(jnp.sum(norm_in[...], axis=0) / CHANNELS + EPS)
    for side in range(2):
        for h in range(4):
            at = side * 512 + h * 128
            for two in range(2):
                emb_ref[two * 8 : two * 8 + 8, at : at + 128] = rows[side, :, two * 4 + h, :] * factors[two]

    partners(sq_out, sq_in, s_sq, r_sq, sent)
    loop(4, lambda i: head(i, sent))
    loop(32, lambda j: result(j, end_either))
    loop(8, lambda w: document(w, end_either))
    loop(32, lambda j: share(j, end_either))


def shards(queries, keys, values, latents, norm_gain, block_doc, block_source):
    dma = pltpu.SemaphoreType.DMA
    hbm = pl.BlockSpec(memory_space=pltpu.HBM)
    vmem = pl.BlockSpec(memory_space=pltpu.VMEM)
    smem = pl.BlockSpec(memory_space=pltpu.SMEM)
    tokens = BLOCKS * BLOCK
    return pl.pallas_call(
        kernel,
        out_shape=(
            jax.ShapeDtypeStruct((256, 1024), BF16),
            jax.ShapeDtypeStruct((DOCS, 1024), F32),
        ),
        in_specs=[smem, smem] + [hbm] * 5,
        out_specs=(vmem, vmem),
        scratch_shapes=[
            pltpu.VMEM((2, BLOCK, 1024), BF16),
            pltpu.VMEM((32, 2 * ROWS, HEAD_DIM), BF16),
            pltpu.VMEM((32, 2 * ROWS, HEAD_DIM), BF16),
            pltpu.VMEM((2, tokens, HEAD_DIM), BF16),
            pltpu.VMEM((512, 512), BF16),
            pltpu.VMEM((4, 128), F32),
            pltpu.VMEM((BLOCKS, BLOCK, 256), BF16),
            pltpu.VMEM((BLOCKS, BLOCK, 256), BF16),
            pltpu.VMEM((BLOCKS, ROWS, 256), BF16),
            pltpu.VMEM((BLOCKS, ROWS, HEAD_DIM), BF16),
            pltpu.VMEM((BLOCKS, ROWS, HEAD_DIM), BF16),
            pltpu.VMEM((32, 2, ROWS, HEAD_DIM), BF16),
            pltpu.VMEM((8, BLOCKS * PIECE), F32),
            pltpu.VMEM((8, 8, BLOCKS * PIECE), F32),
            pltpu.VMEM((8, 8, 128), F32),
            pltpu.VMEM((8, 8, 128), F32),
            pltpu.VMEM((2, 8, 128), F32),
            pltpu.VMEM((4, 2, 8, 128), F32),
            pltpu.VMEM((8, 128), F32),
            pltpu.VMEM((2, 16, 8, 128), F32),
            dma((PARTS, 2, 8)), dma((PARTS, 8)),
            dma((2, PARTS, 8)), dma((2, PARTS, 8)),
            dma((2, PARTS, 8)), dma((2, PARTS, 8)),
            dma((8,)), dma((8,)),
            dma((32,)), dma((32,)),
            dma((2,)), dma((2,)),
            dma,
            dma((32,)), dma((32,)),
            dma((8,)), dma((8,)),
            dma((8,)), dma((8,)),
            dma((4,)), dma((4,)),
            dma((32,)), dma((32,)),
        ],
        compiler_params=pltpu.CompilerParams(
            collective_id=0, has_side_effects=True, vmem_limit_bytes=60 * 1024 * 1024
        ),
        name="embed",
    )(
        block_doc, block_source, queries.reshape(2, BLOCK, 1024), keys, values, latents, norm_gain.reshape(2, 4, 128)
    )


def solution(mesh):
    in_specs = (
        P(("dp", "ctx"), "head"),
        P(("dp", "ctx"), "head"),
        P(("dp", "ctx"), "head"),
        P(None, "head"),
        P("head"),
        P("dp"),
        P("dp"),
    )
    out_specs = (P(("dp", "ctx"), "head"), P("dp", "head"))
    return jax.shard_map(shards, mesh=mesh, in_specs=in_specs, out_specs=out_specs, check_vma=False)
```

time: 108 us -> 97.7 us (0.905)
  Pallas kernels: 99.5 us -> 94.3 us
  local copies, waits for them, and re-layouts: 7.48 us -> 2.53 us
    pallas_call x3 -> x1, Pallas kernels: 99.5 us -> 94.3 us  [shards(): pl.pallas_call(kernel, out_shape=(jax.ShapeDtypeStruct((256, 1024), BF16)...]
    unnamed x16 -> x4, local copies, waits for them, and re-layouts: 7.48 us -> 2.53 us
where the time goes in v3:
time: 97.7 us; the launch traced here: 97.5 us
  Pallas kernels  94.3 us (97%)
  local copies, waits for them, and re-layouts  2.53 us (3%)
    pallas_call x1, Pallas kernels, shards(): pl.pallas_call(kernel, out_shape=(jax.ShapeDtypeStruct((256, 1024), BF16)...  94.3 us
    unnamed x4, local copies, waits for them, and re-layouts  2.53 us

profile of v3, /device:TPU:1, one launch (start us, length us, event | category | flops | bytes accessed | tf_op | source)
XLA Modules:
  0.0 97.5 jit_solution(781191040769210002)
XLA Ops:
  0.6 94.3 %embed.1 = (bf16[256,1024]{1,0:T(8,128)(2,1)}, f32[16,1024]{1,0:T(8,128)}) custom-call(s32[64]{0:T(128)} %doc_ref.1, s32[64]{0:T(128)} %source_ref.1, bf16[2,128,1024]{2,1,0:T(8,128)(2,1)} %bitcast.2, bf16[256,256]{1,0:T(8,128)(2,1)} %k_ref.1, bf16[256,256]{1,0:T(8,128)(2,1)} %v_ref.1, bf16[512,1024]{1,0:T(8,128)(2,1)} %lat_ref.1, f32[2,4,128]{2,1,0:T(4,128)} %bitcast.3), custom_call_target="tpu_custom_call" | custom-call | tf_op jit(solution)/shard_map/embed/pallas_call | solution.py:534
  95.0 0.0 copy-start
  95.0 1.9 %copy.11 = bf16[256,1024]{1,0:T(8,128)(2,1)} copy(bf16[256,1024]{1,0:T(8,128)(2,1)} %get-tuple-element.4) | data formatting | bytes 1048576
  96.9 0.0 copy-done
  96.9 0.6 copy.12
Async XLA Ops:
  95.0 1.9 %copy-start = (f32[16,1024]{1,0:T(8,128)S(1)}, f32[16,1024]{1,0:T(8,128)}, u32[]{:S(2)}) copy-start(f32[16,1024]{1,0:T(8,128)} %get-tuple-element.5) | copy-start | bytes 196612

commit v4 on v3

--- a/solution.py
+++ b/solution.py
@@ -23,6 +23,7 @@
 LONG_KEYS = LONG * BLOCK
 SHORT_KEYS = (BLOCKS - LONG) * BLOCK
 EPS = 1e-05
+OUT_1, OUT_2 = 14, 8
 PARTS = 1
 PART = 256 // PARTS
 HALF = PART // 2
@@ -312,7 +313,6 @@
     loop(32, arrange_queries)
     loop(8, arrange_keys)
 
-    sends_done()
     for copy in pool_inputs()[:2]:
         copy.wait()
 
@@ -414,28 +414,32 @@
         res[p] = o_ref[sorted_place(source_ref[p])]
 
     loop(BLOCKS, move)
-    loop(32, lambda j: result(j, start_either))
-
-    from_partners(sq_in, r_sq)
-    channel_total = jnp.sum(sq_in[...], axis=0)[0:1]
-    factor = lax.rsqrt(channel_total / CHANNELS + EPS)
-    factor = jnp.transpose(jnp.broadcast_to(factor, (128, BLOCKS * PIECE)))
-    whole = o_ref[...].astype(F32).reshape(BLOCKS, 4, PIECE, 128)
-    normed = []
+    def results_out(first_one, count):
+        loop(count, lambda j: result(first_one + j, start_either))
+
+    results_out(0, OUT_1)
+
+    lat = lat_in[...]
+    gained = []
     for h in range(4):
         part = whole[:, h].reshape(BLOCKS * PIECE, 128)
-        normed.append((part * factor * gain_in[h : h + 1, :]).astype(BF16))
-    normed = jnp.concatenate(normed, axis=1)
-
-    lat = lat_in[...]
-    s = lax.dot_general(normed, lat, (((1,), (1,)), ((), ())), preferred_element_type=F32) * 512 ** (-0.5)
-    w = jnp.exp(s - jnp.max(s, axis=-1, keepdims=True))
-    w = (w / jnp.sum(w, axis=-1, keepdims=True)).astype(BF16)
+        gained.append((part * gain_in[h : h + 1, :]).astype(BF16))
+    gained = jnp.concatenate(gained, axis=1)
+    s = lax.dot_general(lat, gained, (((1,), (1,)), ((), ())), preferred_element_type=F32)
     tokens = lax.broadcasted_iota(jnp.int32, (DOCS, PIECE), 0)
     hot = jnp.concatenate(
         [(tokens == doc_ref[packed(i)]).astype(F32) for i in range(BLOCKS)], axis=1
     ).astype(BF16)
-    by_doc = jnp.dot(hot, w, preferred_element_type=F32)
+    sends_done()
+    from_partners(sq_in, r_sq)
+    channel_total = jnp.sum(sq_in[...], axis=0)
+    factor = lax.rsqrt(channel_total / CHANNELS + EPS) * (math.log2(math.e) * 512 ** (-0.5))
+    s = s.reshape(64, 8, BLOCKS * PIECE) * factor[None]
+    top = jnp.max(jnp.max(s, axis=0), axis=0, keepdims=True)
+    w = jnp.exp2(s - top[None])
+    w = w * (1.0 / jnp.sum(jnp.sum(w, axis=0), axis=0, keepdims=True))[None]
+    w = w.reshape(512, BLOCKS * PIECE).astype(BF16)
+    by_doc = lax.dot_general(hot, w, (((1,), (1,)), ((), ())), preferred_element_type=F32)
     sums = None
     for _ in range(3):
         part = by_doc.astype(BF16)
@@ -461,6 +465,7 @@
         )
 
     loop(8, lambda w: document(w, start_either))
+    results_out(OUT_1, OUT_2)
     loop(8, lambda w: arrived(doc_in.at[w], r_d.at[w]))
     row_out[...] = jnp.sum(doc_in[...], axis=0)
 
@@ -475,6 +480,7 @@
         )
 
     loop(32, lambda j: share(j, start_either))
+    results_out(OUT_1 + OUT_2, 32 - OUT_1 - OUT_2)
 
     loop(32, lambda i: arrived(home.at[i], r_o.at[i]))
     for side in range(2):

time: 97.7 us -> 95.6 us (0.979)
  Pallas kernels: 94.3 us -> 92.2 us
    pallas_call x1, Pallas kernels: 94.3 us -> 92.2 us  [shards(): pl.pallas_call(kernel, out_shape=(jax.ShapeDtypeStruct((256, 1024), BF16)...]
where the time goes in v4:
time: 95.6 us; the launch traced here: 95.4 us
  Pallas kernels  92.2 us (96%)
  local copies, waits for them, and re-layouts  2.53 us (3%)
    pallas_call x1, Pallas kernels, shards(): pl.pallas_call(kernel, out_shape=(jax.ShapeDtypeStruct((256, 1024), BF16)...  92.2 us
    unnamed x4, local copies, waits for them, and re-layouts  2.53 us

profile of v4, /device:TPU:1, one launch (start us, length us, event | category | flops | bytes accessed | tf_op | source)
XLA Modules:
  0.0 95.4 jit_solution(17328899371058409872)
XLA Ops:
  0.6 92.2 %embed.1 = (bf16[256,1024]{1,0:T(8,128)(2,1)}, f32[16,1024]{1,0:T(8,128)}) custom-call(s32[64]{0:T(128)} %doc_ref.1, s32[64]{0:T(128)} %source_ref.1, bf16[2,128,1024]{2,1,0:T(8,128)(2,1)} %bitcast.2, bf16[256,256]{1,0:T(8,128)(2,1)} %k_ref.1, bf16[256,256]{1,0:T(8,128)(2,1)} %v_ref.1, bf16[512,1024]{1,0:T(8,128)(2,1)} %lat_ref.1, f32[2,4,128]{2,1,0:T(4,128)} %bitcast.3), custom_call_target="tpu_custom_call" | custom-call | tf_op jit(solution)/shard_map/embed/pallas_call | solution.py:540
  92.9 0.0 copy-start
  92.9 1.9 %copy.11 = bf16[256,1024]{1,0:T(8,128)(2,1)} copy(bf16[256,1024]{1,0:T(8,128)(2,1)} %get-tuple-element.4) | data formatting | bytes 1048576
  94.8 0.0 copy-done
  94.8 0.6 copy.12
Async XLA Ops:
  92.9 1.9 %copy-start = (f32[16,1024]{1,0:T(8,128)S(1)}, f32[16,1024]{1,0:T(8,128)}, u32[]{:S(2)}) copy-start(f32[16,1024]{1,0:T(8,128)} %get-tuple-element.5) | copy-start | bytes 196612

commit v5 on v4

--- a/solution.py
+++ b/solution.py
@@ -17,17 +17,17 @@
 CHANNELS = HEADS * HEAD_DIM
 PIECE = 8
 ROWS = 4 * PIECE
-TILE = 640
+TILE = 1280
 SHORT_TILE = 384
 CHUNK = 256
 LONG_KEYS = LONG * BLOCK
 SHORT_KEYS = (BLOCKS - LONG) * BLOCK
 EPS = 1e-05
-OUT_1, OUT_2 = 14, 8
 PARTS = 1
 PART = 256 // PARTS
 HALF = PART // 2
 AHEAD = 4
+LAY = 2
 Q_START = 4
 Q_STEP = 4
 LAG = 4
@@ -62,6 +62,12 @@
     def worker(self, kv, piece):
         return (kv + 4 * (piece // 8), (piece % 8) // 2, piece % 2)
 
+    def far(self, j):
+        k, i = j // 4, j % 4
+        dz = 4 + (k % 2) * ((k + 1) // 2) - (1 - k % 2) * (k // 2)
+        dy = 2 + (i % 2) * ((i + 1) // 2) - (1 - i % 2) * (i // 2)
+        return (self.z + dz) % 8, (self.y + dy) % 4
+
     def is_me(self, z, y, core):
         return (z == self.z) & (y == self.y) & (core == self.core)
 
@@ -70,7 +76,8 @@
     barrier = pltpu.get_barrier_semaphore()
 
     def one(i):
-        z, y, core = i // 8, (i // 2) % 4, i % 2
+        z, y = me.far(i // 2)
+        core = i % 2
 
         @pl.when(jnp.logical_not(me.is_me(z, y, core)))
         def _():
@@ -120,6 +127,7 @@
     home, sq_out, sq_in, doc_out, doc_in, norm_out, norm_in, row_out, row_in,
     s_a, r_a, s_b, r_b, s_c, r_c, s_s, r_s, s_q, r_q, s_l, r_l, l_q,
     s_o, r_o, s_sq, r_sq, s_d, r_d, s_n, r_n, s_e, r_e,
+    att, l_att,
 ):
     me = Place()
     z, y, core = me.z, me.y, me.core
@@ -217,6 +225,16 @@
     def at_step(e):
         return (z + order(e // PARTS)) % 8, e % PARTS
 
+    def arrange_keys(j):
+        from_z = (z + order(j)) % 8
+        rows = pl.ds(pl.multiple_of(from_z * 1024, 1024), 1024)
+        blocks = pl.ds(from_z * 8, 8)
+        arrived(kv.at[1 - core, rows, :], r_s.at[from_z])
+        key = kv[0, rows, :].reshape(8, BLOCK, 128)
+        ka[blocks, :, 0:128] = key
+        ka[blocks, :, 128:256] = key
+        va[blocks, :, 0:128] = kv[1, rows, :].reshape(8, BLOCK, 128)
+
     def ring(e):
         @pl.when(e < steps)
         def _():
@@ -253,6 +271,10 @@
             @pl.when(part == PARTS - 1)
             def _():
                 to_core(from_z).start()
+
+        @pl.when(e >= 2 * LAG + LAY)
+        def _():
+            arrange_keys(e - 2 * LAG - LAY)
 
     loop(steps + 2 * LAG, ring)
 
@@ -290,16 +312,6 @@
             for copy in pool_inputs()[2:]:
                 copy.wait_send()
 
-    def arrange_keys(j):
-        from_z = (z + order(j)) % 8
-        rows = pl.ds(pl.multiple_of(from_z * 1024, 1024), 1024)
-        blocks = pl.ds(from_z * 8, 8)
-        arrived(kv.at[1 - core, rows, :], r_s.at[from_z])
-        key = kv[0, rows, :].reshape(8, BLOCK, 128)
-        ka[blocks, :, 0:128] = key
-        ka[blocks, :, 128:256] = key
-        va[blocks, :, 0:128] = kv[1, rows, :].reshape(8, BLOCK, 128)
-
     scale = math.log2(math.e) * HEAD_DIM ** (-0.5)
 
     def arrange_queries(s):
@@ -311,7 +323,7 @@
         qa[blocks, :, 128:256] = (query - high.astype(F32)).astype(BF16)
 
     loop(32, arrange_queries)
-    loop(8, arrange_keys)
+    loop(LAY, lambda j: arrange_keys(8 - LAY + j))
 
     for copy in pool_inputs()[:2]:
         copy.wait()
@@ -414,10 +426,7 @@
         res[p] = o_ref[sorted_place(source_ref[p])]
 
     loop(BLOCKS, move)
-    def results_out(first_one, count):
-        loop(count, lambda j: result(first_one + j, start_either))
-
-    results_out(0, OUT_1)
+    loop(32, lambda j: result(j, start_either))
 
     lat = lat_in[...]
     gained = []
@@ -430,7 +439,6 @@
     hot = jnp.concatenate(
         [(tokens == doc_ref[packed(i)]).astype(F32) for i in range(BLOCKS)], axis=1
     ).astype(BF16)
-    sends_done()
     from_partners(sq_in, r_sq)
     channel_total = jnp.sum(sq_in[...], axis=0)
     factor = lax.rsqrt(channel_total / CHANNELS + EPS) * (math.log2(math.e) * 512 ** (-0.5))
@@ -465,22 +473,21 @@
         )
 
     loop(8, lambda w: document(w, start_either))
-    results_out(OUT_1, OUT_2)
     loop(8, lambda w: arrived(doc_in.at[w], r_d.at[w]))
     row_out[...] = jnp.sum(doc_in[...], axis=0)
 
     def share(j, run):
-        s = (j + me.ctx) % 32
+        to_z, to_y = me.far(j)
         dst = row_in.at[half, me.piece]
         slot = half * 16 + me.piece
         run(
-            me.is_me(s // 4, s % 4, home_core),
-            send(row_out, dst, s_e.at[s], r_e.at[slot], me.at(s // 4, s % 4, home_core)),
+            me.is_me(to_z, to_y, home_core),
+            send(row_out, dst, s_e.at[j], r_e.at[slot], me.at(to_z, to_y, home_core)),
             pltpu.make_async_copy(row_out, dst, r_e.at[slot]),
         )
 
     loop(32, lambda j: share(j, start_either))
-    results_out(OUT_1 + OUT_2, 32 - OUT_1 - OUT_2)
+    sends_done()
 
     loop(32, lambda i: arrived(home.at[i], r_o.at[i]))
     for side in range(2):
@@ -491,7 +498,9 @@
                     piece = home[side * 16 + pair * 2 + part, block].astype(F32)
                     rows.append(jnp.concatenate([piece[h * 8 : h * 8 + 8] for h in range(4)], axis=1))
                 at = block * BLOCK + pair * 16
-                att_ref[at : at + 16, side * 512 : side * 512 + 512] = jnp.concatenate(rows, axis=0).astype(BF16)
+                att[at : at + 16, side * 512 : side * 512 + 512] = jnp.concatenate(rows, axis=0).astype(BF16)
+    att_out = pltpu.make_async_copy(att, att_ref, l_att)
+    att_out.start()
 
     loop(32, lambda i: arrived(row_in.at[i // 16, i % 16], r_e.at[i]))
     rows = row_in[...]
@@ -516,6 +525,11 @@
         def _():
             arrived(norm_in.at[i], r_n.at[i])
 
+    partners(sq_out, sq_in, s_sq, r_sq, sent)
+    loop(32, lambda j: result(j, end_either))
+    loop(8, lambda w: document(w, end_either))
+    loop(32, lambda j: share(j, end_either))
+    loop(4, lambda i: head(i, sent))
     loop(4, from_head)
     factors = lax.rsqrt(jnp.sum(norm_in[...], axis=0) / CHANNELS + EPS)
     for side in range(2):
@@ -523,12 +537,7 @@
             at = side * 512 + h * 128
             for two in range(2):
                 emb_ref[two * 8 : two * 8 + 8, at : at + 128] = rows[side, :, two * 4 + h, :] * factors[two]
-
-    partners(sq_out, sq_in, s_sq, r_sq, sent)
-    loop(4, lambda i: head(i, sent))
-    loop(32, lambda j: result(j, end_either))
-    loop(8, lambda w: document(w, end_either))
-    loop(32, lambda j: share(j, end_either))
+    att_out.wait()
 
 
 def shards(queries, keys, values, latents, norm_gain, block_doc, block_source):
@@ -537,14 +546,14 @@
     vmem = pl.BlockSpec(memory_space=pltpu.VMEM)
     smem = pl.BlockSpec(memory_space=pltpu.SMEM)
     tokens = BLOCKS * BLOCK
-    return pl.pallas_call(
+    outs = pl.pallas_call(
         kernel,
         out_shape=(
             jax.ShapeDtypeStruct((256, 1024), BF16),
             jax.ShapeDtypeStruct((DOCS, 1024), F32),
         ),
         in_specs=[smem, smem] + [hbm] * 5,
-        out_specs=(vmem, vmem),
+        out_specs=(hbm, vmem),
         scratch_shapes=[
             pltpu.VMEM((2, BLOCK, 1024), BF16),
             pltpu.VMEM((32, 2 * ROWS, HEAD_DIM), BF16),
@@ -578,6 +587,8 @@
             dma((8,)), dma((8,)),
             dma((4,)), dma((4,)),
             dma((32,)), dma((32,)),
+            pltpu.VMEM((256, 1024), BF16),
+            dma,
         ],
         compiler_params=pltpu.CompilerParams(
             collective_id=0, has_side_effects=True, vmem_limit_bytes=60 * 1024 * 1024
@@ -586,6 +597,44 @@
     )(
         block_doc, block_source, queries.reshape(2, BLOCK, 1024), keys, values, latents, norm_gain.reshape(2, 4, 128)
     )
+    return written(*outs)
+
+
+def out_kernel(att_ref, emb_ref, att_out, emb_out, att, emb, sems_in, sems_out):
+    pieces = [(emb_ref, emb, emb_out)]
+    for i in range(4):
+        rows = pl.ds(64 * i, 64)
+        pieces.append((att_ref.at[rows], att.at[rows], att_out.at[rows]))
+    into = [pltpu.make_async_copy(src, held, sems_in.at[i]) for i, (src, held, _) in enumerate(pieces)]
+    out = [pltpu.make_async_copy(held, dst, sems_out.at[i]) for i, (_, held, dst) in enumerate(pieces)]
+    for copy in into:
+        copy.start()
+    for one, two in zip(into, out):
+        one.wait()
+        two.start()
+    for copy in out:
+        copy.wait()
+
+
+def written(attended, embeddings):
+    hbm = pl.BlockSpec(memory_space=pltpu.HBM)
+    return pl.pallas_call(
+        out_kernel,
+        out_shape=(
+            jax.ShapeDtypeStruct(attended.shape, attended.dtype),
+            jax.ShapeDtypeStruct(embeddings.shape, embeddings.dtype),
+        ),
+        in_specs=[hbm, hbm],
+        out_specs=(hbm, hbm),
+        scratch_shapes=[
+            pltpu.VMEM(attended.shape, attended.dtype),
+            pltpu.VMEM(embeddings.shape, embeddings.dtype),
+            pltpu.SemaphoreType.DMA((5,)),
+            pltpu.SemaphoreType.DMA((5,)),
+        ],
+        compiler_params=pltpu.CompilerParams(vmem_limit_bytes=60 * 1024 * 1024),
+        name="written",
+    )(attended, embeddings)
 
 
 def solution(mesh):

time: 95.6 us -> 91.6 us (0.958)
  local copies, waits for them, and re-layouts: 2.53 us -> 0 us
  Pallas kernels: 92.2 us -> 90.8 us
    pallas_call x1, Pallas kernels: 92.2 us -> 88.9 us  [shards(): pl.pallas_call(kernel, out_shape=(jax.ShapeDtypeStruct((256, 1024), BF16)...]
    unnamed x4 -> x0, local copies, waits for them, and re-layouts: 2.53 us -> none
    pallas_call x0 -> x1, Pallas kernels: none -> 1.87 us  [written(): pl.pallas_call(out_kernel, out_shape=(jax.ShapeDtypeStruct(attended.shape...]
where the time goes in v5:
time: 91.6 us; the launch traced here: 91.4 us
  Pallas kernels  90.8 us (99%)
    pallas_call x1, Pallas kernels, shards(): pl.pallas_call(kernel, out_shape=(jax.ShapeDtypeStruct((256, 1024), BF16)...  88.9 us
    pallas_call x1, Pallas kernels, written(): pl.pallas_call(out_kernel, out_shape=(jax.ShapeDtypeStruct(attended.shape...  1.87 us

profile of v5, /device:TPU:1, one launch (start us, length us, event | category | flops | bytes accessed | tf_op | source)
XLA Modules:
  0.0 91.4 jit_solution(13778740254806856552)
XLA Ops:
  0.6 88.9 %embed.1 = (bf16[256,1024]{1,0:T(8,128)(2,1)}, f32[16,1024]{1,0:T(8,128)}) custom-call(s32[64]{0:T(128)} %doc_ref.1, s32[64]{0:T(128)} %source_ref.1, bf16[2,128,1024]{2,1,0:T(8,128)(2,1)} %bitcast.2, bf16[256,256]{1,0:T(8,128)(2,1)} %k_ref.1, bf16[256,256]{1,0:T(8,128)(2,1)} %v_ref.1, bf16[512,1024]{1,0:T(8,128)(2,1)} %lat_ref.1, f32[2,4,128]{2,1,0:T(4,128)} %bitcast.3), custom_call_target="tpu_custom_call" | custom-call | tf_op jit(solution)/shard_map/embed/pallas_call | solution.py:549
  89.6 1.9 %written.1 = (bf16[256,1024]{1,0:T(8,128)(2,1)}, f32[16,1024]{1,0:T(8,128)}) custom-call(bf16[256,1024]{1,0:T(8,128)(2,1)} %get-tuple-element.4.att_ref, f32[16,1024]{1,0:T(8,128)} %get-tuple-element.5.emb_ref), custom_call_target="tpu_custom_call" | custom-call | tf_op jit(solution)/shard_map/written/pallas_call | solution.py:621

commit v6 on v5

--- a/solution.py
+++ b/solution.py
@@ -18,7 +18,7 @@
 PIECE = 8
 ROWS = 4 * PIECE
 TILE = 1280
-SHORT_TILE = 384
+SHORT_TILE = 256
 CHUNK = 256
 LONG_KEYS = LONG * BLOCK
 SHORT_KEYS = (BLOCKS - LONG) * BLOCK
@@ -155,6 +155,7 @@
         first = jnp.where(doc_ref[i] == doc_ref[i + LONG - 1], i, first)
 
     def packed(i):
+        i = jnp.int32(i)
         return jnp.where(i < LONG, first + i, jnp.where(i - LONG < first, i - LONG, i))
 
     def sorted_place(at):
@@ -276,8 +277,6 @@
         def _():
             arrange_keys(e - 2 * LAG - LAY)
 
-    loop(steps + 2 * LAG, ring)
-
     def pool_inputs():
         other = me.at(z, y, 1 - core)
         half = me.kv % 2
@@ -294,6 +293,9 @@
     def _():
         for copy in pool_inputs():
             copy.start()
+
+    loop(steps + 2 * LAG, ring)
+
 
     def sends_done():
         loop(8, lambda j: column(j, end_either))
@@ -361,18 +363,28 @@
         per = TILE // ROWS
         attend_rows(blocks_of(qa, t * per, per), long_keys, LONG_KEYS // CHUNK, pl.ds(t * per, per))
 
-    def short_keys(c):
-        at = LONG + c * per_chunk
-        docs = [doc_ref[packed(at + b)] for b in range(per_chunk)]
-        return blocks_of(ka, at, per_chunk), blocks_of(va, at, per_chunk), docs
+    reach = BLOCKS - LONG - DOCS + 1
+    per_short = SHORT_TILE // ROWS
+
+    def short_keys(first_chunk):
+        def keys(c):
+            at = LONG + (first_chunk + c) * per_chunk
+            docs = [doc_ref[packed(at + b)] for b in range(per_chunk)]
+            return blocks_of(ka, at, per_chunk), blocks_of(va, at, per_chunk), docs
+
+        return keys
 
     def short_tile(t):
-        per = SHORT_TILE // ROWS
-        at = LONG + t * per
-        docs = jnp.concatenate([jnp.full((ROWS, 128), doc_ref[packed(at + b)], jnp.int32) for b in range(per)], axis=0)
-        attend_rows(blocks_of(qa, at, per), short_keys, SHORT_KEYS // CHUNK, pl.ds(at, per), docs)
-
-    loop((BLOCKS - LONG) * ROWS // SHORT_TILE, short_tile)
+        at = LONG + t * per_short
+        low = max(0, t * per_short - reach) // per_chunk
+        high = -(-min(BLOCKS - LONG, (t + 1) * per_short + reach) // per_chunk)
+        docs = jnp.concatenate(
+            [jnp.full((ROWS, 128), doc_ref[packed(at + b)], jnp.int32) for b in range(per_short)], axis=0
+        )
+        attend_rows(blocks_of(qa, at, per_short), short_keys(low), high - low, pl.ds(at, per_short), docs)
+
+    for t in range((BLOCKS - LONG) // per_short):
+        short_tile(t)
     loop(LONG * ROWS // TILE, long_tile)
 
     whole = o_ref[...].astype(F32).reshape(BLOCKS, 4, PIECE, 128)

time: 91.6 us -> 90.4 us (0.987)
  Pallas kernels: 90.8 us -> 89.6 us
    pallas_call x1, Pallas kernels: 88.9 us -> 87.7 us  [shards(): pl.pallas_call(kernel, out_shape=(jax.ShapeDtypeStruct((256, 1024), BF16)...]
where the time goes in v6:
time: 90.4 us; the launch traced here: 90.2 us
  Pallas kernels  89.6 us (99%)
    pallas_call x1, Pallas kernels, shards(): pl.pallas_call(kernel, out_shape=(jax.ShapeDtypeStruct((256, 1024), BF16)...  87.7 us
    pallas_call x1, Pallas kernels, written(): pl.pallas_call(out_kernel, out_shape=(jax.ShapeDtypeStruct(attended.shape...  1.87 us

profile of v6, /device:TPU:1, one launch (start us, length us, event | category | flops | bytes accessed | tf_op | source)
XLA Modules:
  0.0 90.2 jit_solution(10227888462043652924)
XLA Ops:
  0.6 87.7 %embed.1 = (bf16[256,1024]{1,0:T(8,128)(2,1)}, f32[16,1024]{1,0:T(8,128)}) custom-call(s32[64]{0:T(128)} %doc_ref.1, s32[64]{0:T(128)} %source_ref.1, bf16[2,128,1024]{2,1,0:T(8,128)(2,1)} %bitcast.2, bf16[256,256]{1,0:T(8,128)(2,1)} %k_ref.1, bf16[256,256]{1,0:T(8,128)(2,1)} %v_ref.1, bf16[512,1024]{1,0:T(8,128)(2,1)} %lat_ref.1, f32[2,4,128]{2,1,0:T(4,128)} %bitcast.3), custom_call_target="tpu_custom_call" | custom-call | tf_op jit(solution)/shard_map/embed/pallas_call | solution.py:561
  88.4 1.9 %written.1 = (bf16[256,1024]{1,0:T(8,128)(2,1)}, f32[16,1024]{1,0:T(8,128)}) custom-call(bf16[256,1024]{1,0:T(8,128)(2,1)} %get-tuple-element.4.att_ref, f32[16,1024]{1,0:T(8,128)} %get-tuple-element.5.emb_ref), custom_call_target="tpu_custom_call" | custom-call | tf_op jit(solution)/shard_map/written/pallas_call | solution.py:633
